TPU v7x, 32 devices: a whole 2x2x4 slice. The times are simulated.
32 devices in a mesh: tok: 8 (over z, x), col: 4 (over y, core).
Axes of the slice: x: 2, y: 2, z: 4, core: 2. Of those that a mesh axis runs over, the one named last changes fastest.
Arguments:
- layer_input: bfloat16 [16384, 1024], P('tok', 'col'), may hold values from -6 to 6
- cotangent: bfloat16 [16384, 1024], P('tok', 'col'), may hold values from -9 to 9
- doc_ids: int32 [16384], P('tok'), may hold values from 0 to 2, as said below
- positions: int32 [16384], P('tok'), may hold values from 0 to 2558, as said below
- attn_gain: float32 [1024], replicated, may hold values from 0.1 to 1.9
- mlp_gain: float32 [1024], replicated, may hold values from 0.4 to 2.4
- query_gain: float32 [128], replicated, may hold values from 0.1 to 1.9
- key_norm_gain: float32 [128], replicated, may hold values from 0.1 to 1.9
- query_weight: float32 [2048, 1024], P('col', 'tok'), may hold values from -0.1875 to 0.1875
- key_matrix: float32 [1024, 1024], P('col', 'tok'), may hold values from -0.1875 to 0.1875
- value_matrix: float32 [1024, 1024], P('col', 'tok'), may hold values from -0.1875 to 0.1875
- output_weight: float32 [2048, 1024], P('col', 'tok'), may hold values from -1 to 1
- gate_weight: float32 [3072, 1024], P('col', 'tok'), may hold values from -0.1875 to 0.1875
- up_weight: float32 [3072, 1024], P('col', 'tok')
- down_weight: float32 [3072, 1024], P('col', 'tok')
Outputs:
- layer_output: bfloat16 [16384, 1024], P('tok', 'col')
- input_grad: float32 [16384, 1024], P('tok', 'col')
- attn_gain_grad: float32 [1024], replicated
- mlp_gain_grad: float32 [1024], replicated
- query_gain_grad: float32 [128], replicated
- key_gain_grad: float32 [128], replicated
- query_weight_grad: float32 [2048, 1024], P('col', 'tok')
- key_weight_grad: float32 [1024, 1024], P('col', 'tok')
- value_weight_grad: float32 [1024, 1024], P('col', 'tok')
- output_weight_grad: float32 [2048, 1024], P('col', 'tok')
- gate_weight_grad: float32 [3072, 1024], P('col', 'tok')
- up_weight_grad: float32 [3072, 1024], P('col', 'tok')
- down_weight_grad: float32 [3072, 1024], P('col', 'tok')
Inputs may be any that keep to these rules, and one draw needn't show every extreme that they name: `doc_ids`: within each aligned block of 1024 tokens the ids number the documents from 0 upward and never fall; the tokens with one id in one block form one document, and no document crosses a block's end. `positions`: inside a document the position rises by 1 or 2 from one token to the next.
All inputs are finite; a program needn't handle non-finite values.
Results may differ from a plain program's by a relative error of at most 0.013.
Values may be sent and summed in bfloat16 or wider, within the bound.
No kernel may reach another device: no remote copies, remote signals or barrier semaphores. Data moves between devices by JAX's collectives and lax.ppermute only.
A program may use at most 256 MiB of HBM per device.

v0:
```python
from functools import partial
import math

import jax
import jax.numpy as jnp
from jax import lax
from jax.sharding import PartitionSpec as P

HEAD_WIDTH = 128
SEQ_LEN = 1024


NORM_EPS = 1e-06
ROPE_BASE = 1000000.0
MASK_FILL = -1e30


def contract_last(left, right):
    return lax.dot_general(
        left, right, (((1,), (1,)), ((), ())), preferred_element_type=jnp.float32
    )


def contract_first(left, right):
    return lax.dot_general(
        left, right, (((0,), (0,)), ((), ())), preferred_element_type=jnp.float32
    )


def angle_tables(positions, head_size):
    half_size = head_size // 2
    frequency = jnp.exp(
        jnp.arange(half_size, dtype=jnp.float32) * (-2.0 * math.log(ROPE_BASE) / head_size)
    )
    angles = positions.astype(jnp.float32)[:, None] * frequency[None, :]
    return (jnp.cos(angles), jnp.sin(angles))


def head_norm(values, gain):
    return values * lax.rsqrt(jnp.mean(values * values, axis=-1, keepdims=True) + NORM_EPS) * gain


def rotate(values, cosine_lookup, sine_lookup):
    half_size = values.shape[-1] // 2
    first_half = values[..., :half_size]
    second_half = values[..., half_size:]
    cosine_wide = cosine_lookup[:, None, :]
    sine_wide = sine_lookup[:, None, :]
    return jnp.concatenate(
        [
            first_half * cosine_wide - second_half * sine_wide,
            second_half * cosine_wide + first_half * sine_wide,
        ],
        axis=-1,
    )


def arrange_heads(projected, gain, cosine_lookup, sine_lookup):
    return rotate(head_norm(projected, gain), cosine_lookup, sine_lookup)


def allowed_mask(doc_span):
    span_rows = doc_span.shape[0]
    row_index = jnp.arange(span_rows, dtype=jnp.int32)
    sequence = row_index // SEQ_LEN
    same_doc = doc_span[:, None] == doc_span[None, :]
    same_seq = sequence[:, None] == sequence[None, :]
    return same_doc & same_seq & (row_index[None, :] <= row_index[:, None])


def span_scores(query_span, key_span, allowed):
    span_rows, kv_heads, head_size = key_span.shape
    grouped = query_span.reshape(span_rows, kv_heads, -1, head_size)
    raw_scores = jnp.einsum(
        "qkgd,pkd->kgqp", grouped, key_span, preferred_element_type=jnp.float32
    ) * head_size ** (-0.5)
    return (grouped, jnp.where(allowed[None, None], raw_scores, MASK_FILL))


def attend_span(block):
    query_span, key_span, value_span, doc_span = block
    span_rows = query_span.shape[0]
    grouped, scores = span_scores(query_span, key_span, allowed_mask(doc_span))
    peak_score = jnp.max(scores, axis=-1, keepdims=True)
    expo_scores = jnp.exp(scores - peak_score)
    total_weight = jnp.sum(expo_scores, axis=-1, keepdims=True)
    probs = (expo_scores / total_weight).astype(jnp.bfloat16)
    attended = jnp.einsum("kgqp,pkd->qkgd", probs, value_span, preferred_element_type=jnp.float32)
    log_total = (peak_score + jnp.log(total_weight))[..., 0]
    return (attended.reshape(span_rows, -1).astype(jnp.bfloat16), log_total)


def attend_back(block):
    query_span, key_span, value_span, doc_span, log_total, grad_span = block
    span_rows, kv_heads, head_size = key_span.shape
    allowed = allowed_mask(doc_span)
    grouped, scores = span_scores(query_span, key_span, allowed)
    probs = jnp.where(allowed[None, None], jnp.exp(scores - log_total[..., None]), 0.0)
    grad_heads = grad_span.reshape(span_rows, kv_heads, -1, head_size)
    grad_probs = jnp.einsum(
        "qkgd,pkd->kgqp", grad_heads, value_span, preferred_element_type=jnp.float32
    )
    grad_scores = (
        probs * (grad_probs - jnp.sum(probs * grad_probs, axis=-1, keepdims=True))
    ).astype(jnp.bfloat16)
    scale_factor = head_size ** (-0.5)
    grad_query = (
        jnp.einsum("kgqp,pkd->qkgd", grad_scores, key_span, preferred_element_type=jnp.float32)
        * scale_factor
    )
    grad_key = (
        jnp.einsum("kgqp,qkgd->pkd", grad_scores, grouped, preferred_element_type=jnp.float32)
        * scale_factor
    )
    grad_value = jnp.einsum(
        "kgqp,qkgd->pkd", probs.astype(jnp.bfloat16), grad_heads, preferred_element_type=jnp.float32
    )
    return (grad_query.reshape(span_rows, -1, head_size), grad_key, grad_value.astype(jnp.bfloat16))


def local(
    layer_input,
    cotangent,
    doc_ids,
    positions,
    attn_gain,
    mlp_gain,
    query_gain,
    key_norm_gain,
    query_weight,
    key_matrix,
    value_matrix,
    output_weight,
    gate_weight,
    up_weight,
    down_weight,
):
    count_of_rows, local_width = layer_input.shape
    width = local_width * lax.axis_size("col")
    col_index = lax.axis_index("col")
    col_start = col_index * local_width
    input_rows, cotangent_rows = (
        lax.all_gather(layer_input, "col", axis=1, tiled=True),
        lax.all_gather(cotangent, "col", axis=1, tiled=True),
    )
    full_query, full_key, full_value, full_output, full_gate, full_up, full_down = (
        lax.all_gather(query_weight.astype(jnp.bfloat16), "tok", axis=1, tiled=True),
        lax.all_gather(key_matrix.astype(jnp.bfloat16), "tok", axis=1, tiled=True),
        lax.all_gather(value_matrix.astype(jnp.bfloat16), "tok", axis=1, tiled=True),
        lax.all_gather(output_weight.astype(jnp.bfloat16), "tok", axis=1, tiled=True),
        lax.all_gather(gate_weight.astype(jnp.bfloat16), "tok", axis=1, tiled=True),
        lax.all_gather(up_weight.astype(jnp.bfloat16), "tok", axis=1, tiled=True),
        lax.all_gather(down_weight.astype(jnp.bfloat16), "tok", axis=1, tiled=True),
    )
    input_float = input_rows.astype(jnp.float32)
    inverse_one = lax.rsqrt(jnp.mean(input_float * input_float, axis=-1, keepdims=True) + NORM_EPS)
    normed_one = (input_float * inverse_one * attn_gain).astype(jnp.bfloat16)
    query_heads = contract_last(normed_one, full_query).reshape(count_of_rows, -1, HEAD_WIDTH)
    key_heads = contract_last(normed_one, full_key).reshape(count_of_rows, -1, HEAD_WIDTH)
    value_attention = (
        contract_last(normed_one, full_value)
        .reshape(count_of_rows, -1, HEAD_WIDTH)
        .astype(jnp.bfloat16)
    )
    cosine_lookup, sine_lookup = angle_tables(positions, HEAD_WIDTH)
    prepare_local = partial(arrange_heads, cosine_lookup=cosine_lookup, sine_lookup=sine_lookup)
    query_value, pull_query = jax.vjp(prepare_local, query_heads, query_gain)
    key_value, pull_key = jax.vjp(prepare_local, key_heads, key_norm_gain)
    query_att = query_value.astype(jnp.bfloat16)
    key_attention = key_value.astype(jnp.bfloat16)
    span_rows = math.gcd(count_of_rows // SEQ_LEN, max(1, 512 // SEQ_LEN)) * SEQ_LEN
    span_count = count_of_rows // span_rows

    def to_spans(values):
        return values.reshape((span_count, span_rows) + values.shape[1:])

    attended, log_total = lax.map(
        attend_span,
        (
            to_spans(query_att),
            to_spans(key_attention),
            to_spans(value_attention),
            to_spans(doc_ids),
        ),
    )
    mixed = attended.reshape(count_of_rows, -1)
    attn_part = jnp.dot(mixed, full_output, preferred_element_type=jnp.float32)
    attn_local = lax.psum_scatter(attn_part, "col", scatter_dimension=1, tiled=True)
    residual = layer_input.astype(jnp.float32) + attn_local
    square_sum = lax.psum(jnp.sum(residual * residual, axis=-1), "col")
    inverse_two = lax.rsqrt(square_sum / width + NORM_EPS)[:, None]
    mlp_gain_local = lax.dynamic_slice_in_dim(mlp_gain, col_start, local_width)
    normed_two = lax.all_gather(
        (residual * inverse_two * mlp_gain_local).astype(jnp.bfloat16), "col", axis=1, tiled=True
    )
    gate_proj = contract_last(normed_two, full_gate)
    up_proj = contract_last(normed_two, full_up)
    gate_sigmoid = jax.nn.sigmoid(gate_proj)
    gate_active = gate_proj * gate_sigmoid
    hidden = (gate_active * up_proj).astype(jnp.bfloat16)
    ffn_part = jnp.dot(hidden, full_down, preferred_element_type=jnp.float32)
    ffn_local = lax.psum_scatter(ffn_part, "col", scatter_dimension=1, tiled=True)
    layer_output = (residual + ffn_local).astype(jnp.bfloat16)
    grad_down = contract_first(hidden, cotangent_rows)
    grad_hidden = contract_last(cotangent_rows, full_down)
    grad_gate_act = (
        grad_hidden * up_proj * gate_sigmoid * (1.0 + gate_proj * (1.0 - gate_sigmoid))
    ).astype(jnp.bfloat16)
    grad_up_act = (grad_hidden * gate_active).astype(jnp.bfloat16)
    grad_gate = contract_first(grad_gate_act, normed_two)
    grad_up = contract_first(grad_up_act, normed_two)
    two_part = jnp.dot(grad_gate_act, full_gate, preferred_element_type=jnp.float32) + jnp.dot(
        grad_up_act, full_up, preferred_element_type=jnp.float32
    )
    two_grad = lax.psum_scatter(two_part, "col", scatter_dimension=1, tiled=True)
    scaled_two = two_grad * mlp_gain_local
    inner_two = lax.psum(jnp.sum(scaled_two * residual, axis=-1), "col")
    residual_grad = (
        cotangent.astype(jnp.float32)
        + inverse_two * scaled_two
        - residual * (inverse_two * inverse_two * inverse_two) * (inner_two[:, None] / width)
    )
    mlp_gain_part = lax.dynamic_update_slice(
        jnp.zeros((width,), jnp.float32),
        jnp.sum(two_grad * residual * inverse_two, axis=0),
        (col_start,),
    )
    residual_rows = lax.all_gather(residual_grad.astype(jnp.bfloat16), "col", axis=1, tiled=True)
    grad_output = contract_first(mixed, residual_rows)
    grad_mixed = contract_last(residual_rows, full_output).astype(jnp.bfloat16)
    grad_query_att, grad_key_att, grad_value_att = lax.map(
        attend_back,
        (
            to_spans(query_att),
            to_spans(key_attention),
            to_spans(value_attention),
            to_spans(doc_ids),
            log_total,
            to_spans(grad_mixed),
        ),
    )
    query_back, query_gain_part = pull_query(grad_query_att.reshape(count_of_rows, -1, HEAD_WIDTH))
    key_back, key_gain_part = pull_key(grad_key_att.reshape(count_of_rows, -1, HEAD_WIDTH))
    query_grad_rows = query_back.reshape(count_of_rows, -1).astype(jnp.bfloat16)
    key_grad_rows = key_back.reshape(count_of_rows, -1).astype(jnp.bfloat16)
    value_grad_rows = grad_value_att.reshape(count_of_rows, -1)
    grad_query = contract_first(query_grad_rows, normed_one)
    grad_key = contract_first(key_grad_rows, normed_one)
    grad_value = contract_first(value_grad_rows, normed_one)
    one_part = (
        jnp.dot(query_grad_rows, full_query, preferred_element_type=jnp.float32)
        + jnp.dot(key_grad_rows, full_key, preferred_element_type=jnp.float32)
        + jnp.dot(value_grad_rows, full_value, preferred_element_type=jnp.float32)
    )
    one_local = lax.psum_scatter(one_part, "col", scatter_dimension=1, tiled=True)
    attn_gain_local = lax.dynamic_slice_in_dim(attn_gain, col_start, local_width)
    input_local = layer_input.astype(jnp.float32)
    scaled_local = one_local * attn_gain_local
    inner_one = lax.psum(jnp.sum(scaled_local * input_local, axis=-1), "col")
    input_grad = (
        residual_grad
        + inverse_one * scaled_local
        - input_local * (inverse_one * inverse_one * inverse_one) * (inner_one[:, None] / width)
    )
    attn_gain_part = lax.dynamic_update_slice(
        jnp.zeros((width,), jnp.float32),
        jnp.sum(one_local * input_local * inverse_one, axis=0),
        (col_start,),
    )
    gain_sums = lax.psum(
        (attn_gain_part, mlp_gain_part, query_gain_part, key_gain_part), ("tok", "col")
    )
    sum_query, sum_key, sum_value, sum_output, sum_gate, sum_up, sum_down = (
        lax.psum_scatter(grad_query, "tok", scatter_dimension=1, tiled=True),
        lax.psum_scatter(grad_key, "tok", scatter_dimension=1, tiled=True),
        lax.psum_scatter(grad_value, "tok", scatter_dimension=1, tiled=True),
        lax.psum_scatter(grad_output, "tok", scatter_dimension=1, tiled=True),
        lax.psum_scatter(grad_gate, "tok", scatter_dimension=1, tiled=True),
        lax.psum_scatter(grad_up, "tok", scatter_dimension=1, tiled=True),
        lax.psum_scatter(grad_down, "tok", scatter_dimension=1, tiled=True),
    )
    return (
        layer_output,
        input_grad,
        gain_sums[0],
        gain_sums[1],
        gain_sums[2],
        gain_sums[3],
        sum_query,
        sum_key,
        sum_value,
        sum_output,
        sum_gate,
        sum_up,
        sum_down,
    )


def solution(mesh):
    in_specs = (
        P("tok", "col"),
        P("tok", "col"),
        P("tok"),
        P("tok"),
        P(),
        P(),
        P(),
        P(),
        P("col", "tok"),
        P("col", "tok"),
        P("col", "tok"),
        P("col", "tok"),
        P("col", "tok"),
        P("col", "tok"),
        P("col", "tok"),
    )
    out_specs = (
        P("tok", "col"),
        P("tok", "col"),
        P(),
        P(),
        P(),
        P(),
        P("col", "tok"),
        P("col", "tok"),
        P("col", "tok"),
        P("col", "tok"),
        P("col", "tok"),
        P("col", "tok"),
        P("col", "tok"),
    )
    return jax.shard_map(local, mesh=mesh, in_specs=in_specs, out_specs=out_specs, check_vma=False)
```

profile of v0, /device:TPU:0, one launch (start us, length us, event | category | flops | bytes accessed | tf_op | source)
XLA Modules:
  0.0 1442.6 jit_solution(17161287981474946566)
XLA Ops:
  14.6 29.6 %all_gather.34 = bf16[256,1024]{1,0:T(8,128)(2,1)S(1)} all-gather(bf16[256,128]{1,0:T(8,128)(2,1)S(1)} %convert_element_type.130), channel_id=1, replica_groups=mesh['tok'=8,'col'=4] {'tok'}, dimensions={1}, use_global_device_ids=true | all-gather | bytes 589824 | tf_op jit(solution)/shard_map/all_gather | solution.py:149
  44.2 28.3 %all_gather.35 = bf16[256,1024]{1,0:T(8,128)(2,1)S(1)} all-gather(bf16[256,128]{1,0:T(8,128)(2,1)S(1)} %convert_element_type.133), channel_id=1, replica_groups=mesh['tok'=8,'col'=4] {'tok'}, dimensions={1}, use_global_device_ids=true | all-gather | bytes 589824 | tf_op jit(solution)/shard_map/all_gather | solution.py:148
  137.7 39.6 %while.30 = (s32[]{:T(128)}, bf16[2,1024,512]{2,1,0:T(8,128)(2,1)}, f32[2,2,2,1024]{3,2,1,0:T(2,128)S(1)}, bf16[2,1024,2,128]{3,2,1,0:T(2,128)(2,1)}, s32[2,1024...) while((s32[]{:T(128)}, bf16[2,1024,512]{2,1,0:T(8,128)(2,1)}, ...), condition=%wide.region_6.7_spmd, body=%wide.region_3.6_spmd.sunk | while | flops 2203586560 | bytes 66211956 | solution.py:177
  187.9 66.5 %reduce-scatter.12.cloned.1.call-done = f32[2048,256]{1,0:T(8,128)} async-done(((f32[2048,1024]{1,0:T(8,128)}), f32[2048,256]{1,0:T(8,128)}) %reduce-scatter.12.cloned.1.call-update) | async-done | bytes 2097168 | tf_op jit(solution)/shard_map/reduce_scatter | solution.py:188
  268.6 33.8 %all-gather.20.cloned.1.call-done = bf16[768,1024]{1,0:T(8,128)(2,1)} async-done(((bf16[768,128]{1,0:T(8,128)(2,1)}), bf16[768,1024]{1,0:T(8,128)(2,1)}) %all-gather.20.cloned.1.call-update) | async-done | bytes 1572880 | tf_op jit(solution)/shard_map/all_gather | solution.py:152
  302.4 35.3 %all-gather.16.cloned.1.call-done = bf16[2048,1024]{1,0:T(8,128)(2,1)} async-done(((bf16[2048,256]{1,0:T(8,128)(2,1)}), bf16[2048,1024]{1,0:T(8,128)(2,1)}) %all-gather.16.cloned.1.call-update) | async-done | bytes 4194320 | tf_op jit(solution)/shard_map/all_gather | solution.py:193
  337.7 8.8 fusion.66
  346.5 39.3 %all-gather.18.cloned.1.call-done = bf16[768,1024]{1,0:T(8,128)(2,1)} async-done(((bf16[768,128]{1,0:T(8,128)(2,1)}), bf16[768,1024]{1,0:T(8,128)(2,1)}) %all-gather.18.cloned.1.call-update) | async-done | bytes 1572880 | tf_op jit(solution)/shard_map/all_gather | solution.py:151
  385.9 8.8 fusion.65
  394.7 37.5 %all-gather.22.cloned.1.call-done = bf16[768,1024]{1,0:T(8,128)(2,1)} async-done(((bf16[768,128]{1,0:T(8,128)(2,1)}), bf16[768,1024]{1,0:T(8,128)(2,1)}) %all-gather.22.cloned.1.call-update) | async-done | bytes 1572880 | tf_op jit(solution)/shard_map/all_gather | solution.py:153
  432.2 34.9 %all-gather.24.cloned.1.call-done = bf16[2048,1024]{1,0:T(8,128)(2,1)} async-done(((bf16[2048,256]{1,0:T(8,128)(2,1)}), bf16[2048,1024]{1,0:T(8,128)(2,1)}) %all-gather.24.cloned.1.call-update) | async-done | bytes 4194320 | tf_op jit(solution)/shard_map/all_gather | solution.py:144
  467.1 11.7 multiply_convert_fusion
  488.1 10.0 fusion.67
  498.2 61.7 %reduce-scatter.16.cloned.1.call-done = f32[2048,256]{1,0:T(8,128)} async-done(((f32[2048,1024]{1,0:T(8,128)}), f32[2048,256]{1,0:T(8,128)}) %reduce-scatter.16.cloned.1.call-update) | async-done | bytes 2097168 | tf_op jit(solution)/shard_map/reduce_scatter | solution.py:215
  568.7 65.6 %reduce-scatter.14.cloned.1.call-done = f32[2048,256]{1,0:T(8,128)} async-done(((f32[2048,1024]{1,0:T(8,128)}), f32[2048,256]{1,0:T(8,128)}) %reduce-scatter.14.cloned.1.call-update) | async-done | bytes 2097168 | tf_op jit(solution)/shard_map/reduce_scatter | solution.py:202
  638.4 35.1 %all-gather.26.cloned.1.call-done = bf16[2048,1024]{1,0:T(8,128)(2,1)} async-done(((bf16[2048,256]{1,0:T(8,128)(2,1)}), bf16[2048,1024]{1,0:T(8,128)(2,1)}) %all-gather.26.cloned.1.call-update) | async-done | bytes 4194320 | tf_op jit(solution)/shard_map/all_gather | solution.py:228
  679.8 131.1 %while.31 = (s32[]{:T(128)}, f32[2,1024,4,128]{3,1,0,2:T(8,128)}, f32[2,1024,2,128]{3,1,0,2:T(8,128)}, bf16[2,1024,2,128]{3,2,1,0:T(2,128)(2,1)}, bf16[2,1024,2,...) while((s32[]{:T(128)}, f32[2,1024,4,128]{3,1,0,2:T(8,128)}, ...), condition=%wide.region_16.17_spmd, body=%wide.region_14.16_spmd.sunk | while | flops 5416947712 | bytes 222400848 | solution.py:231
  695.7 14.3 fusion.160
  710.0 9.9 fusion.163
  760.9 14.3 fusion.160
  775.2 9.9 fusion.163
  810.9 8.6 multiply_add_fusion.1
  858.8 9.9 fusion.74
  900.6 21.2 %reduce-scatter.18.cloned.1.call-done = f32[2048,256]{1,0:T(8,128)} async-done(((f32[2048,1024]{1,0:T(8,128)}), f32[2048,256]{1,0:T(8,128)}) %reduce-scatter.18.cloned.1.call-update) | async-done | bytes 2097168 | tf_op jit(solution)/shard_map/reduce_scatter | solution.py:255
  924.8 41.3 %all-reduce.4 = (f32[1024]{0:T(1024)}, f32[1024]{0:T(1024)}, f32[128]{0:T(128)}, f32[128]{0:T(128)}) all-reduce(f32[1024]{0:T(1024)S(1)} %dynamic_update_slice.41, f32[1024]{0:T(1024)S(1)} %dynamic_update_slice.42, f32[128]{0:T(128)S(1)} %get-tuple-element.288, ...), channel_id=1, replica_groups=mesh['tok'=8,'col'=4] {'tok','col'}, use_global_device_ids=true, to_apply=%region_23.24 | all-reduce | flops 2304 | bytes 18432 | tf_op jit(solution)/shard_map/psum | solution.py:270
  976.4 25.7 %reduce-scatter.32.cloned.1.call-done = f32[768,128]{1,0:T(8,128)} async-done(((f32[768,1024]{1,0:T(8,128)}), f32[768,128]{1,0:T(8,128)}) %reduce-scatter.32.cloned.1.call-update) | async-done | bytes 393232 | tf_op jit(solution)/shard_map/reduce_scatter | solution.py:280
  1002.1 78.0 %reduce-scatter.28.cloned.1.call-done = f32[768,128]{1,0:T(8,128)} async-done(((f32[768,1024]{1,0:T(8,128)}), f32[768,128]{1,0:T(8,128)}) %reduce-scatter.28.cloned.1.call-update) | async-done | bytes 393232 | tf_op jit(solution)/shard_map/reduce_scatter | solution.py:278
  1080.1 78.3 %reduce-scatter.30.cloned.1.call-done = f32[768,128]{1,0:T(8,128)} async-done(((f32[768,1024]{1,0:T(8,128)}), f32[768,128]{1,0:T(8,128)}) %reduce-scatter.30.cloned.1.call-update) | async-done | bytes 393232 | tf_op jit(solution)/shard_map/reduce_scatter | solution.py:279
  1158.5 67.0 %reduce-scatter.24.cloned.1.call-done = f32[256,128]{1,0:T(8,128)} async-done(((f32[256,1024]{1,0:T(8,128)}), f32[256,128]{1,0:T(8,128)}) %reduce-scatter.24.cloned.1.call-update) | async-done | bytes 131088 | tf_op jit(solution)/shard_map/reduce_scatter | solution.py:276
  1225.5 67.2 %reduce-scatter.22.cloned.1.call-done = f32[256,128]{1,0:T(8,128)} async-done(((f32[256,1024]{1,0:T(8,128)}), f32[256,128]{1,0:T(8,128)}) %reduce-scatter.22.cloned.1.call-update) | async-done | bytes 131088 | tf_op jit(solution)/shard_map/reduce_scatter | solution.py:275
  1292.7 71.4 %reduce-scatter.26.cloned.1.call-done = f32[512,128]{1,0:T(8,128)} async-done(((f32[512,1024]{1,0:T(8,128)}), f32[512,128]{1,0:T(8,128)}) %reduce-scatter.26.cloned.1.call-update) | async-done | bytes 262160 | tf_op jit(solution)/shard_map/reduce_scatter | solution.py:277
  1364.1 71.3 %reduce-scatter.20.cloned.1.call-done = f32[512,128]{1,0:T(8,128)} async-done(((f32[512,1024]{1,0:T(8,128)}), f32[512,128]{1,0:T(8,128)}) %reduce-scatter.20.cloned.1.call-update) | async-done | bytes 262160 | tf_op jit(solution)/shard_map/reduce_scatter | solution.py:274
  (314 shorter events, 330.9 us)
Async XLA Ops:
  7.2 70.6 %all-gather.10.cloned.1.call-start = ((), (), s32[]{:S(2)}) async-start(), calls=%async_computation.11 | async-start | bytes 5242880 | tf_op jit(solution)/shard_map/all_gather | solution.py:143
  7.9 97.2 %all-gather.12.cloned.1.call-start = ((), (), s32[]{:S(2)}) async-start(), calls=%async_computation.12 | async-start | bytes 1179648 | tf_op jit(solution)/shard_map/all_gather | solution.py:147
  9.6 72.3 %copy-start.43 = (f32[1024]{0:T(1024)S(1)}, f32[1024]{0:T(1024)}, u32[]{:S(2)}) copy-start(f32[1024]{0:T(1024)} %param.23) | copy-start | bytes 12292
  9.6 167.7 %all-gather.14.cloned.1.call-start = ((), (), s32[]{:S(2)}) async-start(), calls=%async_computation.13 | async-start | bytes 1179648 | tf_op jit(solution)/shard_map/all_gather | solution.py:150
  11.3 243.1 %reduce-scatter.12.cloned.1.call-start = ((), (), s32[]{:S(2)}) async-start(), calls=%async_computation.14 | async-start | bytes 10485760 | tf_op jit(solution)/shard_map/reduce_scatter | solution.py:188
  44.2 38.8 %copy-start.20 = (bf16[256,1024]{1,0:T(8,128)(2,1)}, bf16[256,1024]{1,0:T(8,128)(2,1)S(1)}, u32[]{:S(2)}) copy-start(bf16[256,1024]{1,0:T(8,128)(2,1)S(1)} %all_gather.34) | copy-start | bytes 1572868
  77.8 44.1 %copy-start.7 = (f32[2048,64]{1,0:T(8,128)}, f32[2048,64]{1,0:T(8,128)S(1)}, u32[]{:S(2)}) copy-start(f32[2048,64]{1,0:T(8,128)S(1)} %get-tuple-element.354) | copy-start | bytes 1572868
  184.8 69.6 %copy-start.13 = (bf16[2048,256]{1,0:T(8,128)(2,1)S(1)}, bf16[2048,256]{1,0:T(8,128)(2,1)}, u32[]{:S(2)}) copy-start(bf16[2048,256]{1,0:T(8,128)(2,1)} %param.19) | copy-start | bytes 3145732
  184.8 117.6 %all-gather.20.cloned.1.call-start = ((), (), s32[]{:S(2)}) async-start(), calls=%async_computation.17 | async-start | bytes 1769472 | tf_op jit(solution)/shard_map/all_gather | solution.py:152
  186.5 151.2 %all-gather.16.cloned.1.call-start = ((), (), s32[]{:S(2)}) async-start(), calls=%async_computation.15 | async-start | bytes 5242880 | tf_op jit(solution)/shard_map/all_gather | solution.py:193
  187.9 77.4 %copy-start.29 = (f32[768,128]{1,0:T(8,128)S(1)}, f32[768,128]{1,0:T(8,128)}, u32[]{:S(2)}) copy-start(f32[768,128]{1,0:T(8,128)} %param.31) | copy-start | bytes 1179652
  265.2 120.6 %all-gather.18.cloned.1.call-start = ((), (), s32[]{:S(2)}) async-start(), calls=%async_computation.16 | async-start | bytes 1769472 | tf_op jit(solution)/shard_map/all_gather | solution.py:151
  266.0 166.2 %all-gather.22.cloned.1.call-start = ((), (), s32[]{:S(2)}) async-start(), calls=%async_computation.18 | async-start | bytes 1769472 | tf_op jit(solution)/shard_map/all_gather | solution.py:153
  267.8 199.3 %all-gather.24.cloned.1.call-start = ((), (), s32[]{:S(2)}) async-start(), calls=%async_computation.20 | async-start | bytes 5242880 | tf_op jit(solution)/shard_map/all_gather | solution.py:144
  268.5 291.4 %reduce-scatter.16.cloned.1.call-start = ((), (), s32[]{:S(2)}) async-start(), calls=%async_computation.21 | async-start | bytes 10485760 | tf_op jit(solution)/shard_map/reduce_scatter | solution.py:215
  488.1 146.2 %reduce-scatter.14.cloned.1.call-start = ((), (), s32[]{:S(2)}) async-start(), calls=%async_computation.19 | async-start | bytes 10485760 | tf_op jit(solution)/shard_map/reduce_scatter | solution.py:202
  498.1 61.8 %copy-start.42 = (f32[256]{0:T(256)S(1)}, f32[256]{0:T(256)}, u32[]{:S(2)}) copy-start(f32[256]{0:T(256)} %dynamic_slice.71) | copy-start | bytes 3076
  498.2 136.1 %copy-start.19 = (bf16[2048,256]{1,0:T(8,128)(2,1)S(1)}, bf16[2048,256]{1,0:T(8,128)(2,1)}, u32[]{:S(2)}) copy-start(bf16[2048,256]{1,0:T(8,128)(2,1)} %param.20) | copy-start | bytes 3145732
  498.2 136.1 %copy-start.41 = (f32[2048]{0:T(1024)S(1)}, f32[2048]{0:T(1024)}, u32[]{:S(2)}) copy-start(f32[2048]{0:T(1024)} %get-tuple-element.358) | copy-start | bytes 24580
  498.2 175.3 %all-gather.26.cloned.1.call-start = ((), (), s32[]{:S(2)}) async-start(), calls=%async_computation.22 | async-start | bytes 5242880 | tf_op jit(solution)/shard_map/all_gather | solution.py:228
  638.3 283.5 %reduce-scatter.18.cloned.1.call-start = ((), (), s32[]{:S(2)}) async-start(), calls=%async_computation.23 | async-start | bytes 10485760 | tf_op jit(solution)/shard_map/reduce_scatter | solution.py:255
  638.4 41.3 %copy-start.33 = (f32[2,2,2,1024]{3,2,1,0:T(2,128)S(1)}, f32[2,2,2,1024]{3,2,1,0:T(2,128)}, u32[]{:S(2)}) copy-start(f32[2,2,2,1024]{3,2,1,0:T(2,128)} %copy-done.32) | copy-start | bytes 98308
  849.9 152.2 %reduce-scatter.32.cloned.1.call-start = ((), (), s32[]{:S(2)}) async-start(), calls=%async_computation.30 | async-start | bytes 3538944 | tf_op jit(solution)/shard_map/reduce_scatter | solution.py:280
  858.7 221.4 %reduce-scatter.28.cloned.1.call-start = ((), (), s32[]{:S(2)}) async-start(), calls=%async_computation.28 | async-start | bytes 3538944 | tf_op jit(solution)/shard_map/reduce_scatter | solution.py:278
  868.7 289.8 %reduce-scatter.30.cloned.1.call-start = ((), (), s32[]{:S(2)}) async-start(), calls=%async_computation.29 | async-start | bytes 3538944 | tf_op jit(solution)/shard_map/reduce_scatter | solution.py:279
  877.0 348.5 %reduce-scatter.24.cloned.1.call-start = ((), (), s32[]{:S(2)}) async-start(), calls=%async_computation.26 | async-start | bytes 1179648 | tf_op jit(solution)/shard_map/reduce_scatter | solution.py:276
  881.5 411.2 %reduce-scatter.22.cloned.1.call-start = ((), (), s32[]{:S(2)}) async-start(), calls=%async_computation.25 | async-start | bytes 1179648 | tf_op jit(solution)/shard_map/reduce_scatter | solution.py:275
  886.3 477.9 %reduce-scatter.26.cloned.1.call-start = ((), (), s32[]{:S(2)}) async-start(), calls=%async_computation.27 | async-start | bytes 2359296 | tf_op jit(solution)/shard_map/reduce_scatter | solution.py:277
  893.5 28.3 %copy-start.14 = (bf16[2048,256]{1,0:T(8,128)(2,1)S(1)}, bf16[2048,256]{1,0:T(8,128)(2,1)}, u32[]{:S(2)}) copy-start(bf16[2048,256]{1,0:T(8,128)(2,1)} %param.19) | copy-start | bytes 3145732
  893.5 541.8 %reduce-scatter.20.cloned.1.call-start = ((), (), s32[]{:S(2)}) async-start(), calls=%async_computation.24 | async-start | bytes 2359296 | tf_op jit(solution)/shard_map/reduce_scatter | solution.py:274
  899.6 73.6 %copy-start.40 = (f32[2048]{0:T(1024)S(1)}, f32[2048]{0:T(1024)}, u32[]{:S(2)}) copy-start(f32[2048]{0:T(1024)} %get-tuple-element.356) | copy-start | bytes 24580
  921.8 51.4 %copy-start.16 = (f32[2048,256]{1,0:T(8,128)S(1)}, f32[2048,256]{1,0:T(8,128)}, u32[]{:S(2)}) copy-start(f32[2048,256]{1,0:T(8,128)} %reduce-scatter.18.cloned.1.call-done) | copy-start | bytes 6291460
  (53 other events, 404.4 us)
Sparse Core Ops, SparseCore 0:
  9.6 37.7 all-gather.9
  49.9 41.1 all-gather.11
  93.8 38.3 all-gather.13
  184.9 69.4 reduce-scatter.11
  257.1 45.2 all-gather.19
  304.5 33.2 all-gather.15
  340.5 45.2 all-gather.17
  388.7 43.4 all-gather.21
  433.8 33.2 all-gather.23
  488.2 71.6 reduce-scatter.15
  562.5 71.7 reduce-scatter.13
  638.5 35.0 all-gather.25
  850.1 71.7 reduce-scatter.17
  925.9 76.2 reduce-scatter.31
  1006.1 73.9 reduce-scatter.27
  1084.2 74.2 reduce-scatter.29
  1162.3 63.1 reduce-scatter.23
  1229.7 62.9 reduce-scatter.21
  1296.8 67.2 reduce-scatter.25
  1368.1 67.2 reduce-scatter.19
where the time goes:
time: 1450 us; the launch traced here: 1440 us
  waiting for transfers between devices  892 us (62%)
  matrix products  234 us (16%)
  blocking collectives  118 us (8%)
  other arithmetic  106 us (7%)
  local copies, waits for them, and re-layouts  75.1 us (5%)
  between operations  15.5 us (1%)
    reduce_scatter x1, waiting for transfers between devices, local(): lax.psum_scatter(grad_up, 'tok', scatter_dimension=1, tiled=True)  78.3 us
    reduce_scatter x1, waiting for transfers between devices, local(): lax.psum_scatter(grad_gate, 'tok', scatter_dimension=1, tiled=True)  78 us
    reduce_scatter x1, waiting for transfers between devices, local(): lax.psum_scatter(grad_output, 'tok', scatter_dimension=1, tiled=True)  71.4 us
    reduce_scatter x1, waiting for transfers between devices, local(): lax.psum_scatter(grad_query, 'tok', scatter_dimension=1, tiled=True)  71.3 us
    reduce_scatter x1, waiting for transfers between devices, local(): lax.psum_scatter(grad_key, 'tok', scatter_dimension=1, tiled=True)  67.2 us
    reduce_scatter x1, waiting for transfers between devices, local(): lax.psum_scatter(grad_value, 'tok', scatter_dimension=1, tiled=True)  67 us
    reduce_scatter x1, waiting for transfers between devices, local(): lax.psum_scatter(attn_part, 'col', scatter_dimension=1, tiled=True)  66.5 us
    reduce_scatter x1, waiting for transfers between devices, local(): lax.psum_scatter(ffn_part, 'col', scatter_dimension=1, tiled=True)  65.6 us
  transfers between devices with their start and end apart: 20, of which 17 were waited for; matrix products, arithmetic and copies ran while one was open for 14% of the time, Pallas kernels for 0%

commit v1 on v0

v1 whole, which is shorter than its diff:
```python
import math
from functools import partial

import jax
import jax.numpy as jnp
from jax import lax
from jax.experimental import pallas as pl
from jax.experimental.pallas import tpu as pltpu
from jax.sharding import PartitionSpec as P

HEAD = 128
SEQ = 1024
NORM_EPS = 1e-06
ROPE_BASE = 1000000.0
NEG = -1e30
LOG2E = 1.4426950408889634
F32 = jnp.float32
BF16 = jnp.bfloat16
MIB = 1024 * 1024


def dot_nt(a, b):
    return lax.dot_general(a, b, (((1,), (1,)), ((), ())), preferred_element_type=F32)


def dot_nn(a, b):
    return lax.dot_general(a, b, (((1,), (0,)), ((), ())), preferred_element_type=F32)


def dot_tn(a, b):
    return lax.dot_general(a, b, (((0,), (0,)), ((), ())), preferred_element_type=F32)


def call(kernel, grid, ins, outs, args, table=None, scratch=(), flops=0, vmem=40):
    in_specs = [pl.BlockSpec(block, m) for block, m in ins]
    out_specs = [pl.BlockSpec(block, m) for _, _, block, m in outs]
    shapes = [jax.ShapeDtypeStruct(shape, dtype) for shape, dtype, _, _ in outs]
    nbytes = sum(a.size * a.dtype.itemsize for a in args)
    nbytes += sum(math.prod(s.shape) * s.dtype.itemsize for s in shapes)
    spec = pltpu.PrefetchScalarGridSpec(
        num_scalar_prefetch=0 if table is None else 1,
        grid=grid,
        in_specs=in_specs,
        out_specs=out_specs,
        scratch_shapes=list(scratch),
    )
    cost = pl.CostEstimate(flops=int(flops), bytes_accessed=int(nbytes), transcendentals=0)
    run = pl.pallas_call(
        kernel,
        out_shape=shapes,
        grid_spec=spec,
        cost_estimate=cost,
        compiler_params=pltpu.CompilerParams(vmem_limit_bytes=vmem * MIB),
    )
    return run(*args) if table is None else run(table, *args)


def assemble_kernel(slots, tab, a_ref, b_ref, o_ref):
    for p in range(slots):
        lanes = pl.ds(pl.multiple_of(tab[3 * p + 1] * 128, 128), 128)
        here = pl.ds(p * 128, 128)

        @pl.when(tab[3 * p + 2] == 0)
        def _():
            o_ref[:, here] = a_ref[tab[3 * p], :, lanes]

        @pl.when(tab[3 * p + 2] != 0)
        def _():
            o_ref[:, here] = b_ref[tab[3 * p], :, lanes]


def assemble_norm_kernel(slots, tab, a_ref, b_ref, gain_ref, x_ref, n_ref):
    assemble_kernel(slots, tab, a_ref, b_ref, x_ref)
    x = x_ref[...].astype(F32)
    r = lax.rsqrt(jnp.mean(x * x, axis=-1, keepdims=True) + NORM_EPS)
    n_ref[...] = (x * r * gain_ref[...]).astype(BF16)


def rope(u, cos, sin):
    return u * cos + pltpu.roll(u, HEAD // 2, axis=1) * sin


def rope_back(d, cos, sin):
    return d * cos - pltpu.roll(d, HEAD // 2, axis=1) * sin


def project_kernel(groups, n_ref, w_ref, cos_ref, sin_ref, qg_ref, kg_ref, o_ref, u_ref, r_ref):
    n = n_ref[...]
    cos, sin = cos_ref[...], sin_ref[...]
    lane = lax.broadcasted_iota(jnp.int32, (n.shape[0], 128), 1)
    inverses = jnp.zeros((n.shape[0], 128), F32)
    for g in range(groups):
        out = dot_nt(n, w_ref[pl.ds(g * 512, 512), :])
        for i in range(3):
            u = out[:, i * 128 : (i + 1) * 128]
            r = lax.rsqrt(jnp.mean(u * u, axis=-1, keepdims=True) + NORM_EPS)
            u = u * r
            gain = qg_ref[...] if i < 2 else kg_ref[...]
            o_ref[:, pl.ds(g * 512 + i * 128, 128)] = rope(u * gain, cos, sin).astype(BF16)
            u_ref[:, pl.ds(g * 384 + i * 128, 128)] = u.astype(BF16)
            inverses = jnp.where(lane == g * 3 + i, r, inverses)
        o_ref[:, pl.ds(g * 512 + 384, 128)] = out[:, 384:].astype(BF16)
    r_ref[...] = inverses


def visible(start_ref, first, rows, last):
    start = start_ref[:, pl.ds(first, rows)]
    start = jnp.concatenate([start, start], axis=1)
    key = lax.broadcasted_iota(jnp.int32, (last, 2 * rows), 0)
    query = lax.broadcasted_iota(jnp.int32, (1, 2 * rows), 1)
    query = jnp.where(query >= rows, query - rows, query) + first
    return (key >= start) & (key <= query)


def attend_kernel(rows, qkv_ref, start_ref, o_ref, l_ref):
    scale = HEAD**-0.5 * LOG2E
    for i in range(SEQ // rows):
        first, last = i * rows, (i + 1) * rows
        span = pl.ds(first, rows)
        q = jnp.concatenate([qkv_ref[span, 0:128], qkv_ref[span, 128:256]], axis=0)
        s = dot_nt(qkv_ref[0:last, 256:384], q) * scale
        s = jnp.where(visible(start_ref, first, rows, last), s, NEG)
        m = jnp.max(s, axis=0, keepdims=True)
        e = jnp.exp2(s - m)
        total = jnp.sum(e, axis=0, keepdims=True)
        o = dot_tn(qkv_ref[0:last, 384:512], e.astype(BF16)) * (1.0 / total)
        o = o.T.astype(BF16)
        o_ref[span, 0:128] = o[:rows]
        o_ref[span, 128:256] = o[rows:]
        log_total = m + jnp.log2(total)
        l_ref[0, 0:1, span] = log_total[:, :rows]
        l_ref[0, 1:2, span] = log_total[:, rows:]


def attend_back_kernel(
    rows, qkv_ref, do_ref, l_ref, start_ref, u_ref, r_ref, cos_ref, sin_ref, qg_ref, kg_ref,
    o_ref, gain_ref, dk_ref, dv_ref,
):
    g = pl.program_id(0)
    scale = HEAD**-0.5

    @pl.when(g == 0)
    def _():
        gain_ref[...] = jnp.zeros_like(gain_ref)

    lane = lax.broadcasted_iota(jnp.int32, (SEQ, 128), 1)

    def through(grad, head, span, gain):
        u = u_ref[span, pl.ds(head * 128, 128)].astype(F32)
        picked = jnp.where(lane[: grad.shape[0]] == g * 3 + head, r_ref[span, :], 0.0)
        r = jnp.sum(picked, axis=-1, keepdims=True)
        d = rope_back(grad, cos_ref[span, :], sin_ref[span, :])
        gain_part = jnp.sum(d * u, axis=0, keepdims=True)
        d = d * gain
        d = r * (d - u * jnp.mean(u * d, axis=-1, keepdims=True))
        return d.astype(BF16), gain_part

    q_part = jnp.zeros((1, HEAD), F32)
    for i in reversed(range(SEQ // rows)):
        first, last = i * rows, (i + 1) * rows
        span = pl.ds(first, rows)
        keys = pl.ds(0, last)
        q = jnp.concatenate([qkv_ref[span, 0:128], qkv_ref[span, 128:256]], axis=0)
        do = jnp.concatenate([do_ref[span, 0:128], do_ref[span, 128:256]], axis=0)
        log_total = jnp.concatenate([l_ref[0, 0:1, span], l_ref[0, 1:2, span]], axis=1)
        k = qkv_ref[0:last, 256:384]
        s = dot_nt(k, q) * (scale * LOG2E)
        s = jnp.where(visible(start_ref, first, rows, last), s, NEG)
        p = jnp.exp2(s - log_total)
        t = p * dot_nt(qkv_ref[0:last, 384:512], do)
        ds = (t - p * jnp.sum(t, axis=0, keepdims=True)).astype(BF16)
        dv = dot_nn(p.astype(BF16), do)
        dk = dot_nn(ds, q)
        if last == SEQ:
            dv_ref[...] = dv
            dk_ref[...] = dk
        else:
            dv_ref[keys, :] += dv
            dk_ref[keys, :] += dk
        dq = (dot_tn(k, ds) * scale).T
        for head in range(2):
            out, part = through(dq[head * rows : (head + 1) * rows], head, span, qg_ref[...])
            o_ref[span, pl.ds(head * 128, 128)] = out
            q_part += part
    out, k_part = through(dk_ref[...] * scale, 2, pl.ds(0, SEQ), kg_ref[...])
    o_ref[:, 256:384] = out
    o_ref[:, 384:512] = dv_ref[...].astype(BF16)
    gain_ref[0:1, :] += q_part
    gain_ref[1:2, :] += k_part


def residual_kernel(parts, x_ref, *refs):
    total = x_ref[...].astype(F32)
    for ref in refs[:parts]:
        total += ref[...].astype(F32)
    gain_ref, res_ref, n_ref = refs[parts:]
    r = lax.rsqrt(jnp.mean(total * total, axis=-1, keepdims=True) + NORM_EPS)
    res_ref[...] = total
    n_ref[...] = (total * r * gain_ref[...]).astype(BF16)


def ffn_kernel(n_ref, c_ref, wg_ref, wu_ref, wd_ref, h_ref, dg_ref, du_ref, f_ref, t_ref):
    n = n_ref[...]
    gate = dot_nt(n, wg_ref[...])
    up = dot_nt(n, wu_ref[...])
    dh = dot_nt(c_ref[...], wd_ref[...])
    sig = 1.0 / (1.0 + jnp.exp2(gate * -LOG2E))
    act = gate * sig
    hidden = (act * up).astype(BF16)
    du = (dh * act).astype(BF16)
    dg = (dh * up * sig * (1.0 + gate * (1.0 - sig))).astype(BF16)
    h_ref[...] = hidden
    dg_ref[...] = dg
    du_ref[...] = du
    f_ref[...] = dot_nn(hidden, wd_ref[...]).astype(BF16)
    t_ref[...] = (dot_nn(dg, wg_ref[...]) + dot_nn(du, wu_ref[...])).astype(BF16)


def sum_parts(whole, halves, tab):
    total = None
    for ref in whole:
        part = ref[...].astype(F32)
        total = part if total is None else total + part
    if halves:
        per = pl.num_programs(0) // 2
        mine = pl.program_id(0) // per == tab[0]
        total += jnp.where(mine, halves[0][...].astype(F32), halves[1][...].astype(F32))
    return total


def pick_blocks(count, tab, base, source, own_ref, send_ref):
    for which, ref in enumerate((own_ref, send_ref)):
        for i in range(count):
            at = tab[base + which * count + i]
            lanes = pl.ds(pl.multiple_of(at * 128, 128), 128)
            ref[:, i * 128 : (i + 1) * 128] = source[:, lanes].astype(ref.dtype)


def middle_kernel(whole, half, tab, res_ref, cot_ref, gain_ref, *refs):
    two = sum_parts(refs[:whole], refs[whole : whole + half], tab)
    dres_ref, low_ref, part_ref = refs[whole + half :]
    res = res_ref[...]
    width = res.shape[-1]
    r = lax.rsqrt(jnp.mean(res * res, axis=-1, keepdims=True) + NORM_EPS)
    scaled = two * gain_ref[...]
    inner = jnp.sum(scaled * res, axis=-1, keepdims=True)
    grad = cot_ref[...].astype(F32) + r * scaled - res * (r * r * r * (inner / width))
    dres_ref[...] = grad
    low_ref[...] = grad.astype(BF16)

    @pl.when(pl.program_id(0) == 0)
    def _():
        part_ref[...] = jnp.zeros_like(part_ref)

    part_ref[...] += jnp.sum(two * res * r, axis=0, keepdims=True)


def output_kernel(whole, half, count, tab, res_ref, *refs):
    total = sum_parts(refs[:whole], refs[whole : whole + half], tab)
    own_ref, send_ref, hold = refs[whole + half :]
    hold[...] = res_ref[...] + total
    pick_blocks(count, tab, 1, hold, own_ref, send_ref)


def final_kernel(whole, half, count, tab, x_ref, dres_ref, gain_ref, *refs):
    one = sum_parts(refs[:whole], refs[whole : whole + half], tab)
    own_ref, send_ref, part_ref, hold = refs[whole + half :]
    x = x_ref[...].astype(F32)
    width = x.shape[-1]
    r = lax.rsqrt(jnp.mean(x * x, axis=-1, keepdims=True) + NORM_EPS)
    scaled = one * gain_ref[...]
    inner = jnp.sum(scaled * x, axis=-1, keepdims=True)
    hold[...] = dres_ref[...] + r * scaled - x * (r * r * r * (inner / width))
    pick_blocks(count, tab, 1, hold, own_ref, send_ref)

    @pl.when(pl.program_id(0) == 0)
    def _():
        part_ref[...] = jnp.zeros_like(part_ref)

    part_ref[...] += jnp.sum(one * x * r, axis=0, keepdims=True)


def grad_kernel(pairs, *refs):
    total = None
    for i in range(pairs):
        part = dot_tn(refs[2 * i][...], refs[2 * i + 1][...])
        total = part if total is None else total + part
    lo_ref, hi_ref = refs[2 * pairs :]
    half = lo_ref.shape[-1]
    lo_ref[...] = total[:, :half].astype(BF16)
    hi_ref[...] = total[:, half:].astype(BF16)


def weight_grad(pairs, first, count, block=256):
    rows, width = pairs[0][1].shape
    block = min(block, count)
    base = first // block
    ins, args = [], []
    for a, b in pairs:
        ins += [((rows, block), lambda i: (0, base + i)), ((rows, width), lambda i: (0, 0))]
        args += [a, b]
    out = ((count, width // 2), BF16, (block, width // 2), lambda i: (i, 0))
    return call(
        partial(grad_kernel, len(pairs)),
        (count // block,),
        ins,
        [out, out],
        args,
        flops=2 * rows * count * width * len(pairs),
    )


def ffn(n, cot, cot_first, w_gate, w_up, w_down, block=256):
    rows, width = n.shape
    hidden = w_gate.shape[0]
    base = cot_first // block
    row = ((block, width), lambda i: (i, 0))
    weight = ((hidden, width), lambda i: (0, 0))
    inner = ((rows, hidden), BF16, (block, hidden), lambda i: (i, 0))
    outer = ((rows, width), BF16, (block, width), lambda i: (i, 0))
    return call(
        ffn_kernel,
        (rows // block,),
        [row, ((block, width), lambda i: (base + i, 0)), weight, weight, weight],
        [inner, inner, inner, outer, outer],
        [n, cot, w_gate, w_up, w_down],
        flops=12 * rows * width * hidden,
        vmem=48,
    )


def row_specs(parts, halves, block, width, rows):
    per = rows // block // 2
    ins = [((block, width), lambda i, *_: (i, 0)) for _ in parts]
    ins += [((block, width), lambda i, *_: (i % per, 0)) for _ in halves]
    return ins


def local(
    layer_input, cotangent, doc_ids, positions, attn_gain, mlp_gain, query_gain, key_norm_gain,
    query_weight, key_matrix, value_matrix, output_weight, gate_weight, up_weight, down_weight,
):
    rows, lane_width = layer_input.shape
    nt, nc = lax.axis_size("tok"), lax.axis_size("col")
    width = lane_width * nc
    half = nc // 2
    tok, col = lax.axis_index("tok"), lax.axis_index("col")
    dp, tp = col // half, col % half
    fast = nt == 8 and nc == 4 and width // nt == 128
    chunks = lane_width // 128

    def swap_dp(a):
        return lax.ppermute(a, "col", [(j, (j + half) % nc) for j in range(nc)])

    def swap_core(a):
        return lax.ppermute(a, "col", [(j, j ^ 1) for j in range(nc)])

    groups = [[d * half + t for t in range(half)] for d in range(2)]

    def sum_tp(a):
        return lax.psum(a.astype(F32), "col", axis_index_groups=groups)

    def swap_x(a):
        return lax.ppermute(a, "tok", [(t, t ^ 1) for t in range(nt)])

    def from_z(a, k):
        return lax.ppermute(a, "tok", [(t, ((t // 2 - k) % 4) * 2 + t % 2) for t in range(nt)])

    def to_z(a, k):
        return lax.ppermute(a, "tok", [(t, ((t // 2 + k) % 4) * 2 + t % 2) for t in range(nt)])

    if fast:
        z, x = tok // 2, tok % 2
        order = [((z + p % 4) % 4) * 2 + (x ^ (p // 4)) for p in range(8)]

        def slot_of(t):
            return ((t % 2) ^ x) * 4 + (t // 2 - z) % 4

        pieces = nt
    else:
        pieces = width // 128
        order = list(range(pieces))

        def slot_of(t):
            return t

    def arrange(v):
        parts = [lax.dynamic_slice(v, (128 * t,), (128,)) for t in order]
        return jnp.concatenate(parts)[None, :]

    def restore(v):
        return jnp.concatenate(
            [lax.dynamic_slice(v, (128 * slot_of(t),), (128,)) for t in range(pieces)]
        )

    out_table = [tp]
    for block in (col, (col + half) % nc):
        out_table += [slot_of(block * chunks + i) for i in range(chunks)]
    out_table = jnp.stack([jnp.asarray(t, jnp.int32) for t in out_table])

    kv_rows = key_matrix.shape[0] // HEAD
    mixed_weight = []
    for g in range(kv_rows):
        mixed_weight += [
            query_weight[g * 256 : (g + 1) * 256],
            key_matrix[g * 128 : (g + 1) * 128],
            value_matrix[g * 128 : (g + 1) * 128],
        ]
    own_qkv = jnp.concatenate(mixed_weight, axis=0).astype(BF16)
    own_out = output_weight.astype(BF16)
    own_up = jnp.concatenate([gate_weight, up_weight], axis=0).astype(BF16)
    own_down = down_weight.astype(BF16)
    hidden = gate_weight.shape[0]

    if fast:

        def gather_z(p):
            return [p] + [from_z(p, k) for k in (1, 2, 3)]

        def gather(p):
            return jnp.concatenate((own := gather_z(p)) + [swap_x(q) for q in own], axis=1)

        def gather_x_last(p):
            own = gather_z(p)
            other = [swap_dp(q) for q in own]
            own, other = own + [swap_x(q) for q in own], other + [swap_x(q) for q in other]
            return jnp.concatenate(
                [jnp.concatenate(own, axis=1), jnp.concatenate(other, axis=1)], axis=0
            )

        def gather_y_last(p):
            own = gather_z(p)
            own = own + [swap_x(q) for q in own]
            other = [swap_dp(q) for q in own]
            return jnp.concatenate(
                [jnp.concatenate(own, axis=1), jnp.concatenate(other, axis=1)], axis=0
            )

    else:

        def gather(p):
            return lax.all_gather(p, "tok", axis=1, tiled=True)

        def gather_x_last(p):
            own = gather(p)
            return jnp.concatenate([own, swap_dp(own)], axis=0)

        gather_y_last = gather_x_last

    gain_one, gain_two = arrange(attn_gain), arrange(mlp_gain)

    def seq_rows(a, which):
        return lax.dynamic_slice_in_dim(a, which * SEQ, SEQ, axis=0)

    if fast:
        in_table = []
        for t in order:
            block = t // chunks
            in_table += [
                (block // half != dp).astype(jnp.int32),
                t % chunks,
                (block % half != tp).astype(jnp.int32),
            ]
        in_table = jnp.stack(in_table)
        got = swap_dp(seq_rows(layer_input, 1 - dp))
        mine = jnp.stack([seq_rows(layer_input, dp), got])
        other = swap_core(mine)
        spec = ((2, 256, lane_width), lambda i, *_: (0, i, 0))
        row = ((SEQ, width), BF16, (256, width), lambda i, *_: (i, 0))
        x_rows, normed_one = call(
            partial(assemble_norm_kernel, pieces),
            (SEQ // 256,),
            [spec, spec, ((1, width), lambda i, *_: (0, 0))],
            [row, row],
            [mine, other, gain_one],
            table=in_table,
        )
        cot_mine = jnp.stack([cotangent, swap_dp(cotangent)])
        cot_other = swap_core(cot_mine)

        def cot_map(i, tab):
            d, t = tab[24], tab[25]
            return (0, jnp.where(i < 2, d * 2 + i, (1 - d) * 2 + (i - 2 + t) % 2), 0)

        spec = ((2, 512, lane_width), cot_map)
        cot_rows = call(
            partial(assemble_kernel, pieces),
            (4,),
            [spec, spec],
            [((2 * SEQ, width), BF16, (512, width), lambda i, *_: (i, 0))],
            [cot_mine, cot_other],
            table=jnp.concatenate([in_table, jnp.stack([dp, tp]).astype(jnp.int32)]),
        )[0]
    else:
        whole_input = lax.all_gather(layer_input, "col", axis=1, tiled=True)
        whole_cot = lax.all_gather(cotangent, "col", axis=1, tiled=True)
        x_rows = seq_rows(whole_input, dp)
        cot_rows = jnp.concatenate([seq_rows(whole_cot, dp), seq_rows(whole_cot, 1 - dp)], axis=0)
        wide = x_rows.astype(F32)
        inverse = lax.rsqrt(jnp.mean(wide * wide, axis=-1, keepdims=True) + NORM_EPS)
        normed_one = (wide * inverse * gain_one).astype(BF16)

    place = lax.dynamic_slice_in_dim(positions, dp * SEQ, SEQ).astype(F32)
    steps = jnp.arange(HEAD // 2, dtype=F32)
    frequency = jnp.exp(steps * (-2.0 * math.log(ROPE_BASE) / HEAD))
    angle = place[:, None] * frequency[None, :]
    cosine, sine = jnp.cos(angle), jnp.sin(angle)
    cosine = jnp.concatenate([cosine, cosine], axis=1)
    sine = jnp.concatenate([-sine, sine], axis=1)
    docs = lax.dynamic_slice_in_dim(doc_ids, dp * SEQ, SEQ)
    start = jnp.sum((docs[:, None] < docs[None, :]).astype(jnp.int32), axis=0)[None, :]
    query_row, key_row = query_gain[None, :], key_norm_gain[None, :]

    w_qkv = gather_x_last(own_qkv)
    count = w_qkv.shape[0] // 512
    row = lambda i, *_: (i, 0)
    fixed = lambda i, *_: (0, 0)
    by_head = lambda i, *_: (0, i)
    qkv, unit, inverses = call(
        partial(project_kernel, count),
        (SEQ // 256,),
        [
            ((256, width), row),
            ((count * 512, width), fixed),
            ((256, 128), row),
            ((256, 128), row),
            ((1, 128), fixed),
            ((1, 128), fixed),
        ],
        [
            ((SEQ, count * 512), BF16, (256, count * 512), row),
            ((SEQ, count * 384), BF16, (256, count * 384), row),
            ((SEQ, 128), F32, (256, 128), row),
        ],
        [normed_one, w_qkv, cosine, sine, query_row, key_row],
        flops=2 * SEQ * width * count * 512,
    )
    head_block = lambda n: ((SEQ, n), by_head)
    log_block = ((1, 2, SEQ), lambda i, *_: (i, 0, 0))
    mixed, log_total = call(
        partial(attend_kernel, 256),
        (count,),
        [head_block(512), ((1, SEQ), fixed)],
        [
            ((SEQ, count * 256), BF16, (SEQ, 256), by_head),
            ((count, 2, SEQ), F32, (1, 2, SEQ), lambda i, *_: (i, 0, 0)),
        ],
        [qkv, start],
        flops=8 * SEQ * SEQ * HEAD * count,
    )
    w_out = gather_y_last(own_out)
    out_part = dot_nn(mixed, w_out)
    if fast:
        out_part = out_part.astype(BF16)
        parts = [out_part, swap_core(out_part)]
    else:
        parts = [sum_tp(out_part)]
    residual, normed_two = call(
        partial(residual_kernel, len(parts)),
        (SEQ // 256,),
        [((256, width), row)] * (1 + len(parts)) + [((1, width), fixed)],
        [
            ((SEQ, width), F32, (256, width), row),
            ((SEQ, width), BF16, (256, width), row),
        ],
        [x_rows, *parts, gain_two],
    )

    if fast:
        piece = lax.dynamic_slice_in_dim(normed_two, tp * (SEQ // 2), SEQ // 2, axis=0)
        piece = swap_dp(piece)
        normed_other = jnp.concatenate([piece, swap_core(piece)], axis=0)
    else:
        normed_other = swap_dp(normed_two)
    w_both = gather(own_up)
    w_gate, w_up = w_both[:hidden], w_both[hidden:]
    w_down = gather(own_down)
    hid_a, gate_a, up_a, ffn_a, two_a = ffn(normed_two, cot_rows, 0, w_gate, w_up, w_down)
    hid_b, gate_b, up_b, ffn_b, two_b = ffn(normed_other, cot_rows, SEQ, w_gate, w_up, w_down)

    if fast:

        def collect(a, b):
            mid = SEQ // 2
            mine = (b[:mid].astype(F32) + swap_core(b[mid:]).astype(F32)).astype(BF16)
            got = swap_dp(mine)
            return [a, swap_core(a)], [got, swap_core(got)]
    else:

        def collect(a, b):
            return [sum_tp(a) + swap_dp(sum_tp(b))], []

    whole, halves = collect(two_a, two_b)
    d_res, d_low, mlp_part = call(
        partial(middle_kernel, len(whole), len(halves)),
        (SEQ // 256,),
        [((256, width), row), ((256, width), row), ((1, width), fixed)]
        + row_specs(whole, halves, 256, width, SEQ),
        [
            ((SEQ, width), F32, (256, width), row),
            ((SEQ, width), BF16, (256, width), row),
            ((1, width), F32, (1, width), fixed),
        ],
        [residual, cot_rows, gain_two, *whole, *halves],
        table=out_table,
    )

    whole, halves = collect(ffn_a, ffn_b)
    own_y, send_y = call(
        partial(output_kernel, len(whole), len(halves), chunks),
        (SEQ // 256,),
        [((256, width), row)] + row_specs(whole, halves, 256, width, SEQ),
        [((SEQ, lane_width), BF16, (256, lane_width), row)] * 2,
        [residual, *whole, *halves],
        table=out_table,
        scratch=[pltpu.VMEM((256, width), F32)],
    )

    def by_sequence(own, other):
        return jnp.where(
            dp == 0,
            jnp.concatenate([own, other], axis=0),
            jnp.concatenate([other, own], axis=0),
        )

    layer_output = by_sequence(own_y, swap_dp(send_y))

    cot_a, cot_b = cot_rows[:SEQ], cot_rows[SEQ:]
    grad_down = weight_grad([(hid_a, cot_a), (hid_b, cot_b)], 0, hidden)
    grad_gate = weight_grad([(gate_a, normed_two), (gate_b, normed_other)], 0, hidden)
    grad_up = weight_grad([(up_a, normed_two), (up_b, normed_other)], 0, hidden)

    d_mixed = dot_nt(d_low, w_out).astype(BF16)
    out_rows = mixed.shape[1] // 2
    grad_out_own = weight_grad([(mixed, d_low)], 0, out_rows)
    grad_out_other = weight_grad([(mixed, d_low)], out_rows, out_rows)
    d_qkv, gain_part = call(
        partial(attend_back_kernel, 256),
        (count,),
        [
            head_block(512),
            head_block(256),
            log_block,
            ((1, SEQ), fixed),
            head_block(384),
            ((SEQ, 128), fixed),
            ((SEQ, 128), fixed),
            ((SEQ, 128), fixed),
            ((1, 128), fixed),
            ((1, 128), fixed),
        ],
        [
            ((SEQ, count * 512), BF16, (SEQ, 512), by_head),
            ((8, 128), F32, (8, 128), fixed),
        ],
        [qkv, d_mixed, log_total, start, unit, inverses, cosine, sine, query_row, key_row],
        scratch=[pltpu.VMEM((SEQ, 128), F32), pltpu.VMEM((SEQ, 128), F32)],
        flops=20 * SEQ * SEQ * HEAD * count,
    )
    one_part = dot_nn(d_qkv, w_qkv)
    if fast:
        one_part = one_part.astype(BF16)
        whole = [one_part, swap_core(one_part)]
    else:
        whole = [sum_tp(one_part)]
    own_x, send_x, attn_part = call(
        partial(final_kernel, len(whole), 0, chunks),
        (SEQ // 256,),
        [((256, width), row), ((256, width), row), ((1, width), fixed)]
        + row_specs(whole, [], 256, width, SEQ),
        [
            ((SEQ, lane_width), F32, (256, lane_width), row),
            ((SEQ, lane_width), BF16, (256, lane_width), row),
            ((1, width), F32, (1, width), fixed),
        ],
        [x_rows, d_res, gain_one, *whole],
        table=out_table,
        scratch=[pltpu.VMEM((256, width), F32)],
    )
    input_grad = by_sequence(own_x, swap_dp(send_x).astype(F32))
    qkv_rows = d_qkv.shape[1] // 2
    grad_qkv_own = weight_grad([(d_qkv, normed_one)], 0, qkv_rows)
    grad_qkv_other = weight_grad([(d_qkv, normed_one)], qkv_rows, qkv_rows)

    if fast:

        def add(a, b):
            return a.astype(F32) + b.astype(F32)

        def low_add(a, b):
            return add(a, b).astype(BF16)

        def sum_z(a):
            return a[:, :128].astype(F32) + sum(
                to_z(a[:, 128 * k : 128 * (k + 1)], k).astype(F32) for k in (1, 2, 3)
            )

        def scatter(g):
            lo, hi = g
            return sum_z(low_add(lo, swap_x(hi)))

        def scatter_x_first(own, other):
            own = low_add(own[0], swap_x(own[1]))
            other = low_add(other[0], swap_x(other[1]))
            return sum_z(low_add(own, swap_dp(other)))

        def scatter_y_first(own, other):
            lo = low_add(own[0], swap_dp(other[0]))
            hi = low_add(own[1], swap_dp(other[1]))
            return sum_z(low_add(lo, swap_x(hi)))

    else:

        def scatter(g):
            wide_grad = jnp.concatenate(g, axis=1).astype(F32)
            return lax.psum_scatter(wide_grad, "tok", scatter_dimension=1, tiled=True)

        def scatter_x_first(own, other):
            own = jnp.concatenate(own, axis=1).astype(F32)
            own += swap_dp(jnp.concatenate(other, axis=1)).astype(F32)
            return lax.psum_scatter(own, "tok", scatter_dimension=1, tiled=True)

        scatter_y_first = scatter_x_first

    sum_down, sum_gate, sum_up = scatter(grad_down), scatter(grad_gate), scatter(grad_up)
    sum_out = scatter_y_first(grad_out_own, grad_out_other)
    sum_qkv = scatter_x_first(grad_qkv_own, grad_qkv_other)
    sum_qkv = sum_qkv.reshape(kv_rows, 512, -1)
    sum_query = sum_qkv[:, :256].reshape(kv_rows * 256, -1)
    sum_key = sum_qkv[:, 256:384].reshape(kv_rows * 128, -1)
    sum_value = sum_qkv[:, 384:].reshape(kv_rows * 128, -1)

    share = 1.0 / half
    gains = lax.psum(
        jnp.concatenate(
            [
                restore(attn_part[0]) * share,
                restore(mlp_part[0]) * share,
                gain_part[0],
                gain_part[1],
            ]
        ),
        ("tok", "col"),
    )
    return (
        layer_output,
        input_grad,
        gains[:width],
        gains[width : 2 * width],
        gains[2 * width : 2 * width + 128],
        gains[2 * width + 128 :],
        sum_query,
        sum_key,
        sum_value,
        sum_out,
        sum_gate,
        sum_up,
        sum_down,
    )


def solution(mesh):
    rows, cols, both, every = P("tok"), P("col", "tok"), P("tok", "col"), P()
    in_specs = (both, both, rows, rows, every, every, every, every) + (cols,) * 7
    out_specs = (both, both, every, every, every, every) + (cols,) * 7
    return jax.shard_map(local, mesh=mesh, in_specs=in_specs, out_specs=out_specs, check_vma=False)
```

time: 1450 us -> 582 us (0.40)
  waiting for transfers between devices: 892 us -> 190 us
  matrix products: 234 us -> 15.7 us
  Pallas kernels: 0 us -> 121 us
  starting transfers between devices: 1.29 us -> 113 us
  blocking collectives: 118 us -> 38.5 us
  other arithmetic: 106 us -> 34.9 us
  local copies, waits for them, and re-layouts: 75.1 us -> 59.1 us
    reduce_scatter x11 -> x0, waiting for transfers between devices: 674 us -> none  [the longest x1 78.3 us: local(): lax.psum_scatter(grad_up, 'tok', scatter_dimension=1, tiled=True)]
    dot_general x35 -> x3, matrix products: 234 us -> 15.7 us  [the longest x2 13.3 us: dot_nn(): lax.dot_general(a, b, (((1,), (0,)), ((), ())), preferred_element_type=F32)]
    all_gather x9 -> x0, waiting for transfers between devices: 216 us -> none  [the longest x1 39.3 us: local(): lax.all_gather(gate_weight.astype(jnp.bfloat16), 'tok', axis=1, tiled=True)]
    ppermute x0 -> x86, waiting for transfers between devices: none -> 190 us  [the longest x26 96.3 us: swap_x(): return lax.ppermute(a, 'tok', [(t, t ^ 1) for t in range(nt)])]
    pallas_call x0 -> x18, Pallas kernels: none -> 121 us  [call(): return run(*args) if table is None else run(table, *args)]
    ppermute x0 -> x86, starting transfers between devices: none -> 113 us  [the longest x15 32.3 us: to_z(): lax.ppermute(a, 'tok', [(t, (t // 2 + k) % 4 * 2 + t % 2) for t in range(...]
    all_gather x2 -> x0, blocking collectives: 57.8 us -> none  [the longest x1 29.6 us: local(): lax.all_gather(value_matrix.astype(jnp.bfloat16), 'tok', axis=1, tiled=True)]
    unnamed x102 -> x184, local copies, waits for them, and re-layouts: 7.35 us -> 43.5 us
  transfers between devices with their start and end apart: 20 -> 86, of which waited for: 17 -> 37; matrix products, arithmetic and copies ran while one was open for 14% -> 14% of each run, Pallas kernels for 0% -> 18%
where the time goes in v1:
time: 582 us; the launch traced here: 575 us
  waiting for transfers between devices  190 us (33%)
  Pallas kernels  121 us (21%)
  starting transfers between devices  113 us (19%)
  local copies, waits for them, and re-layouts  59.1 us (10%)
  blocking collectives  38.5 us (7%)
  other arithmetic  34.9 us (6%)
  matrix products  15.7 us (3%)
    pallas_call x18, Pallas kernels, call(): return run(*args) if table is None else run(table, *args)  121 us
    ppermute x26, waiting for transfers between devices, swap_x(): return lax.ppermute(a, 'tok', [(t, t ^ 1) for t in range(nt)])  96.3 us
    unnamed x184, local copies, waits for them, and re-layouts  43.5 us
    psum x1, blocking collectives, local(): lax.psum(jnp.concatenate([restore(attn_part[0]) * share, restore(mlp_part...  38.5 us
    ppermute x15, waiting for transfers between devices, to_z(): lax.ppermute(a, 'tok', [(t, (t // 2 + k) % 4 * 2 + t % 2) for t in range(...  37.4 us
    ppermute x15, starting transfers between devices, to_z(): lax.ppermute(a, 'tok', [(t, (t // 2 + k) % 4 * 2 + t % 2) for t in range(...  32.3 us
    ppermute x26, starting transfers between devices, swap_x(): return lax.ppermute(a, 'tok', [(t, t ^ 1) for t in range(nt)])  31.8 us
    ppermute x22, waiting for transfers between devices, swap_dp(): return lax.ppermute(a, 'col', [(j, (j + half) % nc) for j in range(nc)])  29.7 us
  transfers between devices with their start and end apart: 86, of which 37 were waited for; matrix products, arithmetic and copies ran while one was open for 14% of the time, Pallas kernels for 18%

profile of v1, /device:TPU:0, one launch (start us, length us, event | category | flops | bytes accessed | tf_op | source)
XLA Modules:
  0.0 574.6 jit_solution(3265913907415685047)
XLA Ops:
  7.3 5.0 collective-permute-start.2
  35.7 4.8 collective-permute-done.18
  57.5 8.0 %collective-permute-done.25 = bf16[512,128]{1,0:T(8,128)(2,1)S(1)} collective-permute-done((bf16[512,128]{1,0:T(8,128)(2,1)S(1)}, bf16[512,128]{1,0:T(8,128)(2,1)S(1)}, u32[]{:S(2)}, u32[]{:S(2)}) %collective-permute-start.25) | collective-permute-done | bytes 131104 | tf_op jit(solution)/shard_map/ppermute | solution.py:353
  78.3 6.4 %collective-permute-done.29 = bf16[512,128]{1,0:T(8,128)(2,1)S(1)} collective-permute-done((bf16[512,128]{1,0:T(8,128)(2,1)S(1)}, bf16[512,128]{1,0:T(8,128)(2,1)S(1)}, u32[]{:S(2)}, u32[]{:S(2)}) %collective-permute-start.29) | collective-permute-done | bytes 131104 | tf_op jit(solution)/shard_map/ppermute | solution.py:353
  107.7 4.1 collective-permute-done.8
  113.3 4.1 collective-permute-done.14
  132.1 9.0 %shard_map.247 = (bf16[1024,2048]{1,0:T(8,128)(2,1)S(1)}, bf16[1024,1536]{1,0:T(8,128)(2,1)S(1)}, f32[1024,128]{1,0:T(8,128)S(1)}) custom-call(bf16[1024,1024]{1,0:T(8,128)(2,1)S(1)} %get-tuple-element.57.n_ref.refs_1_, bf16[2048,1024]{1,0:T(8,128)(2,1)} %pad_maximum_fusion.w_ref, f32[1024,128]{1,0:T(8,128)S(1)} %get-tuple-element.151.cos_ref, ...), custom_call_target="tpu_custom_call" | custom-call | flops 4294967296 | bytes 15205376 | tf_op jit(solution)/shard_map/pallas_call | solution.py:55
  141.2 11.1 %shard_map.248 = (bf16[1024,1024]{1,0:T(8,128)(2,1)S(1)}, f32[4,2,1024]{2,1,0:T(2,128)S(1)}) custom-call(bf16[1024,2048]{1,0:T(8,128)(2,1)S(1)} %get-tuple-element.58.qkv_ref, s32[1,1024]{1,0:T(1,128)S(1)} %bitcast.119), custom_call_target="tpu_custom_call" | custom-call | flops 4294967296 | bytes 6328320 | tf_op jit(solution)/shard_map/pallas_call | solution.py:55
  174.1 21.5 %collective-permute-done.36 = bf16[1536,128]{1,0:T(8,128)(2,1)S(1)} collective-permute-done((bf16[1536,128]{1,0:T(8,128)(2,1)}, bf16[1536,128]{1,0:T(8,128)(2,1)S(1)}, u32[]{:S(2)}, u32[]{:S(2)}) %collective-permute-start.36) | collective-permute-done | bytes 393248 | tf_op jit(solution)/shard_map/ppermute | solution.py:367
  217.6 7.6 %collective-permute-done.40 = bf16[1536,128]{1,0:T(8,128)(2,1)S(1)} collective-permute-done((bf16[1536,128]{1,0:T(8,128)(2,1)S(1)}, bf16[1536,128]{1,0:T(8,128)(2,1)S(1)}, u32[]{:S(2)}, u32[]{:S(2)}) %collective-permute-start.40) | collective-permute-done | bytes 393248 | tf_op jit(solution)/shard_map/ppermute | solution.py:364
  225.9 7.2 %collective-permute-done.41 = bf16[1536,128]{1,0:T(8,128)(2,1)S(1)} collective-permute-done((bf16[1536,128]{1,0:T(8,128)(2,1)S(1)}, bf16[1536,128]{1,0:T(8,128)(2,1)S(1)}, u32[]{:S(2)}, u32[]{:S(2)}) %collective-permute-start.41) | collective-permute-done | bytes 393248 | tf_op jit(solution)/shard_map/ppermute | solution.py:364
  242.4 14.4 %shard_map.251 = (bf16[1024,768]{1,0:T(8,128)(2,1)S(1)}, bf16[1024,768]{1,0:T(8,128)(2,1)S(1)}, bf16[1024,768]{1,0:T(8,128)(2,1)S(1)}, bf16[1024,1024]{1,0:T(8,128)(2,1)}, bf16[1024,1024]{1,0:T(8,128)(2,1)}) custom-call(bf16[1024,1024]{1,0:T(8,128)(2,1)} %copy-done.12, bf16[2048,1024]{1,0:T(8,128)(2,1)} %copy-done, ...), custom_call_target="tpu_custom_call" | custom-call | flops 9663676416 | bytes 19922944 | tf_op jit(solution)/shard_map/pallas_call | solution.py:55
  261.8 14.4 %shard_map.252 = (bf16[1024,768]{1,0:T(8,128)(2,1)S(1)}, bf16[1024,768]{1,0:T(8,128)(2,1)S(1)}, bf16[1024,768]{1,0:T(8,128)(2,1)S(1)}, bf16[1024,1024]{1,0:T(8,128)(2,1)}, bf16[1024,1024]{1,0:T(8,128)(2,1)}) custom-call(bf16[1024,1024]{1,0:T(8,128)(2,1)} %copy-done.14, bf16[2048,1024]{1,0:T(8,128)(2,1)} %copy-done, ...), custom_call_target="tpu_custom_call" | custom-call | flops 9663676416 | bytes 19922944 | tf_op jit(solution)/shard_map/pallas_call | solution.py:55
  279.9 4.8 shard_map.263
  294.1 4.1 shard_map.262
  298.5 4.1 shard_map.261
  308.9 13.3 %collective-permute-done.78 = bf16[768,512]{1,0:T(8,128)(2,1)S(1)} collective-permute-done((bf16[768,512]{1,0:T(8,128)(2,1)S(1)}, bf16[768,512]{1,0:T(8,128)(2,1)S(1)}, u32[]{:S(2)}, u32[]{:S(2)}) %collective-permute-start.78) | collective-permute-done | bytes 786464 | tf_op jit(solution)/shard_map/ppermute | solution.py:364
  326.0 11.8 %collective-permute-done.74 = bf16[768,512]{1,0:T(8,128)(2,1)S(1)} collective-permute-done((bf16[768,512]{1,0:T(8,128)(2,1)S(1)}, bf16[768,512]{1,0:T(8,128)(2,1)S(1)}, u32[]{:S(2)}, u32[]{:S(2)}) %collective-permute-start.74) | collective-permute-done | bytes 786464 | tf_op jit(solution)/shard_map/ppermute | solution.py:364
  343.9 6.4 %collective-permute-done.84 = bf16[768,128]{1,0:T(8,128)(2,1)S(1)} collective-permute-done((bf16[768,128]{1,0:T(8,128)(2,1)S(1)}, bf16[768,128]{1,0:T(8,128)(2,1)S(1)}, u32[]{:S(2)}, u32[]{:S(2)}) %collective-permute-start.84) | collective-permute-done | bytes 196640 | tf_op jit(solution)/shard_map/ppermute | solution.py:370
  355.3 5.2 collective-permute-done.79
  362.4 5.5 collective-permute-done.80
  379.7 5.4 collective-permute-done.76
  387.6 6.2 %shard_map.254 = (f32[1024,1024]{1,0:T(8,128)S(1)}, bf16[1024,1024]{1,0:T(8,128)(2,1)S(1)}, f32[1,1024]{1,0:T(1,128)S(1)}) custom-call(s32[5]{0:T(128)S(1)} %stack.168.tab, f32[1024,1024]{1,0:T(8,128)} %copy-done.1, bf16[2048,1024]{1,0:T(8,128)(2,1)} %copy-done, f32[1,1024]{1,0:T(1,128)S(1)} %bitcast.118, bf16[1024,1024]{1,0:T(8,128)(2,1)S(1)} %copy-done.5, ...), custom_call_target="tpu_custom_call" | custom-call | bytes 20979712 | tf_op jit(solution)/shard_map/pallas_call | solution.py:55
  400.7 21.2 %shard_map.255 = (bf16[1024,2048]{1,0:T(8,128)(2,1)S(1)}, f32[8,128]{1,0:T(8,128)S(1)}) custom-call(bf16[1024,2048]{1,0:T(8,128)(2,1)} %copy-done.32, bf16[1024,1024]{1,0:T(8,128)(2,1)S(1)} %convolution_convert_fusion.1.do_ref, f32[4,2,1024]{2,1,0:T(2,128)S(1)} %get-tuple-element.70.l_ref, s32[1,1024]{1,0:T(1,128)S(1)} %bitcast.120, ...), custom_call_target="tpu_custom_call" | custom-call | flops 10737418240 | bytes 15246336 | tf_op jit(solution)/shard_map/pallas_call | solution.py:55
  430.9 4.2 shard_map.257
  435.1 9.7 %convolution_convert_fusion.refs_0_ = bf16[1024,1024]{1,0:T(8,128)(2,1)} fusion(bf16[1024,2048]{1,0:T(8,128)(2,1)} %copy-done.21, bf16[1024,1024]{1,0:T(8,128)(2,1)} %copy-done.38, bf16[1024,1024]{1,0:T(8,128)(2,1)} %copy-done.39), kind=kOutput, calls=%fused_computation.10 | convolution fusion | flops 4304404480 | bytes 10485760 | tf_op jit(solution)/shard_map/dot_general | solution.py:27
  445.2 5.2 shard_map.253
  459.0 29.0 %collective-permute-done.70 = bf16[512,512]{1,0:T(8,128)(2,1)S(1)} collective-permute-done((bf16[512,512]{1,0:T(8,128)(2,1)S(1)}, bf16[512,512]{1,0:T(8,128)(2,1)S(1)}, u32[]{:S(2)}, u32[]{:S(2)}) %collective-permute-start.70) | collective-permute-done | bytes 524320 | tf_op jit(solution)/shard_map/ppermute | solution.py:364
  492.4 5.3 collective-permute-done.71
  514.0 5.4 shard_map.256
  520.4 38.5 %psum.7 = f32[2304]{0:T(1024)S(1)} all-reduce(f32[2304]{0:T(1024)S(1)} %pad_maximum_fusion.9), channel_id=1, replica_groups=mesh['tok'=8,'col'=4] {'tok','col'}, use_global_device_ids=true, to_apply=%region_1.2 | all-reduce | flops 2304 | bytes 18432 | tf_op jit(solution)/shard_map/psum | solution.py:734
  564.9 7.6 %collective-permute-done.61 = bf16[1024,256]{1,0:T(8,128)(2,1)S(1)} collective-permute-done((bf16[1024,256]{1,0:T(8,128)(2,1)}, bf16[1024,256]{1,0:T(8,128)(2,1)S(1)}, u32[]{:S(2)}, u32[]{:S(2)}) %collective-permute-start.61) | collective-permute-done | bytes 524320 | tf_op jit(solution)/shard_map/ppermute | solution.py:353
  (417 shorter events, 261.6 us)
Async XLA Ops:
  7.3 44.2 %collective-permute-start.2 = (bf16[1024,128]{1,0:T(8,128)(2,1)}, bf16[1024,128]{1,0:T(8,128)(2,1)}, u32[]{:S(2)}, u32[]{:S(2)}) collective-permute-start(bf16[1024,128]{1,0:T(8,128)(2,1)} %get-tuple-element.133), channel_id=1, source_target_pairs={{0,24},{4,28},{8,0},{12,4},{16,8},{20,12},{24,16},{28,20},{1,25},{... | collective-permute-start | bytes 786440 | tf_op jit(solution)/shard_map/ppermute | solution.py:367
  12.4 35.8 %collective-permute-start.9 = (bf16[1024,128]{1,0:T(8,128)(2,1)}, bf16[1024,128]{1,0:T(8,128)(2,1)}, u32[]{:S(2)}, u32[]{:S(2)}) collective-permute-start(bf16[1024,128]{1,0:T(8,128)(2,1)} %get-tuple-element.133), channel_id=1, source_target_pairs={{0,2},{1,3},{2,0},{3,1},{4,6},{5,7},{6,4},{7,5},{8,10},{9,11},{10,... | collective-permute-start | bytes 786440 | tf_op jit(solution)/shard_map/ppermute | solution.py:353
  13.9 39.1 %collective-permute-start.3 = (bf16[1024,128]{1,0:T(8,128)(2,1)}, bf16[1024,128]{1,0:T(8,128)(2,1)}, u32[]{:S(2)}, u32[]{:S(2)}) collective-permute-start(bf16[1024,128]{1,0:T(8,128)(2,1)} %get-tuple-element.133), channel_id=1, source_target_pairs={{0,16},{4,20},{8,24},{12,28},{16,0},{20,4},{24,8},{28,12},{1,17},{... | collective-permute-start | bytes 786440 | tf_op jit(solution)/shard_map/ppermute | solution.py:367
  48.1 43.7 %collective-permute-start = (bf16[1024,256]{1,0:T(8,128)(2,1)}, bf16[1024,256]{1,0:T(8,128)(2,1)S(1)}, u32[]{:S(2)}, u32[]{:S(2)}) collective-permute-start(bf16[1024,256]{1,0:T(8,128)(2,1)} %get-tuple-element.111), channel_id=1, source_target_pairs={{0,2},{1,3},{2,0},{3,1},{4,6},{5,7},{6,4},{7,5},{8,10},{9,11},{10,... | collective-permute-start | bytes 1572872 | tf_op jit(solution)/shard_map/ppermute | solution.py:353
  51.5 105.3 %collective-permute-start.42 = (bf16[768,128]{1,0:T(8,128)(2,1)}, bf16[768,128]{1,0:T(8,128)(2,1)}, u32[]{:S(2)}, u32[]{:S(2)}) collective-permute-start(bf16[768,128]{1,0:T(8,128)(2,1)} %get-tuple-element.100), channel_id=1, source_target_pairs={{0,24},{4,28},{8,0},{12,4},{16,8},{20,12},{24,16},{28,20},{1,25},{... | collective-permute-start | bytes 589832 | tf_op jit(solution)/shard_map/ppermute | solution.py:367
  98.5 30.9 %collective-permute-start.1 = (bf16[2,1024,256]{2,1,0:T(8,128)(2,1)S(1)}, bf16[2,1024,256]{2,1,0:T(8,128)(2,1)S(1)}, u32[]{:S(2)}, u32[]{:S(2)}) collective-permute-start(bf16[2,1024,256]{2,1,0:T(8,128)(2,1)S(1)} %pad_maximum_fusion.5.a_ref), channel_id=1, source_target_pairs={{0,1},{1,0},{2,3},{3,2},{4,5},{5,4},{6,7},{7,6},{8,9},{9,8},{10,11... | collective-permute-start | bytes 3145736 | tf_op jit(solution)/shard_map/ppermute | solution.py:356
  117.4 43.9 %collective-permute-start.43 = (bf16[768,128]{1,0:T(8,128)(2,1)}, bf16[768,128]{1,0:T(8,128)(2,1)S(1)}, u32[]{:S(2)}, u32[]{:S(2)}) collective-permute-start(bf16[768,128]{1,0:T(8,128)(2,1)} %get-tuple-element.100), channel_id=1, source_target_pairs={{0,16},{4,20},{8,24},{12,28},{16,0},{20,4},{24,8},{28,12},{1,17},{... | collective-permute-start | bytes 589832 | tf_op jit(solution)/shard_map/ppermute | solution.py:367
  121.4 41.5 %collective-permute-start.44 = (bf16[768,128]{1,0:T(8,128)(2,1)}, bf16[768,128]{1,0:T(8,128)(2,1)}, u32[]{:S(2)}, u32[]{:S(2)}) collective-permute-start(bf16[768,128]{1,0:T(8,128)(2,1)} %get-tuple-element.100), channel_id=1, source_target_pairs={{0,8},{4,12},{8,16},{12,20},{16,24},{20,28},{24,0},{28,4},{1,9},{5... | collective-permute-start | bytes 589832 | tf_op jit(solution)/shard_map/ppermute | solution.py:367
  124.9 46.7 %collective-permute-start.33 = (bf16[2048,256]{1,0:T(8,128)(2,1)}, bf16[2048,256]{1,0:T(8,128)(2,1)}, u32[]{:S(2)}, u32[]{:S(2)}) collective-permute-start(bf16[2048,256]{1,0:T(8,128)(2,1)} %param.16), channel_id=1, source_target_pairs={{0,2},{1,3},{2,0},{3,1},{4,6},{5,7},{6,4},{7,5},{8,10},{9,11},{10,... | collective-permute-start | bytes 3145736 | tf_op jit(solution)/shard_map/ppermute | solution.py:353
  156.0 54.8 %collective-permute-start.32 = (bf16[1024,1024]{1,0:T(8,128)(2,1)}, bf16[1024,1024]{1,0:T(8,128)(2,1)}, u32[]{:S(2)}, u32[]{:S(2)}) collective-permute-start(bf16[1024,1024]{1,0:T(8,128)(2,1)} %convolution_convert_fusion.2.refs_0_), channel_id=1, source_target_pairs={{0,1},{1,0},{2,3},{3,2},{4,5},{5,4},{6,7},{7,6},{8,9},{9,8},{10,11... | collective-permute-start | bytes 6291464 | tf_op jit(solution)/shard_map/ppermute | solution.py:356
  162.9 32.6 %collective-permute-start.36 = (bf16[1536,128]{1,0:T(8,128)(2,1)}, bf16[1536,128]{1,0:T(8,128)(2,1)S(1)}, u32[]{:S(2)}, u32[]{:S(2)}) collective-permute-start(bf16[1536,128]{1,0:T(8,128)(2,1)} %get-tuple-element.126), channel_id=1, source_target_pairs={{0,16},{4,20},{8,24},{12,28},{16,0},{20,4},{24,8},{28,12},{1,17},{... | collective-permute-start | bytes 1179656 | tf_op jit(solution)/shard_map/ppermute | solution.py:367
  169.4 29.5 %collective-permute-start.38 = (bf16[1536,128]{1,0:T(8,128)(2,1)}, bf16[1536,128]{1,0:T(8,128)(2,1)S(1)}, u32[]{:S(2)}, u32[]{:S(2)}) collective-permute-start(bf16[1536,128]{1,0:T(8,128)(2,1)} %get-tuple-element.126), channel_id=1, source_target_pairs={{0,4},{4,0},{8,12},{12,8},{16,20},{20,16},{24,28},{28,24},{1,5},{5... | collective-permute-start | bytes 1179656 | tf_op jit(solution)/shard_map/ppermute | solution.py:364
  171.7 28.4 %collective-permute-start.46 = (bf16[768,128]{1,0:T(8,128)(2,1)}, bf16[768,128]{1,0:T(8,128)(2,1)S(1)}, u32[]{:S(2)}, u32[]{:S(2)}) collective-permute-start(bf16[768,128]{1,0:T(8,128)(2,1)} %collective-permute-done.42), channel_id=1, source_target_pairs={{0,4},{4,0},{8,12},{12,8},{16,20},{20,16},{24,28},{28,24},{1,5},{5... | collective-permute-start | bytes 589832 | tf_op jit(solution)/shard_map/ppermute | solution.py:364
  195.5 42.4 %collective-permute-start.34 = (bf16[2,2048,256]{2,1,0:T(8,128)(2,1)S(1)}, bf16[2,2048,256]{2,1,0:T(8,128)(2,1)S(1)}, u32[]{:S(2)}, u32[]{:S(2)}) collective-permute-start(bf16[2,2048,256]{2,1,0:T(8,128)(2,1)S(1)} %pad_maximum_fusion.2.a_ref), channel_id=1, source_target_pairs={{0,1},{1,0},{2,3},{3,2},{4,5},{5,4},{6,7},{7,6},{8,9},{9,8},{10,11... | collective-permute-start | bytes 6291464 | tf_op jit(solution)/shard_map/ppermute | solution.py:356
  287.6 100.0 %collective-permute-start.56 = (bf16[1024,1024]{1,0:T(8,128)(2,1)}, bf16[1024,1024]{1,0:T(8,128)(2,1)S(1)}, u32[]{:S(2)}, u32[]{:S(2)}) collective-permute-start(bf16[1024,1024]{1,0:T(8,128)(2,1)} %get-tuple-element.66.refs_0_), channel_id=1, source_target_pairs={{0,1},{1,0},{2,3},{3,2},{4,5},{5,4},{6,7},{7,6},{8,9},{9,8},{10,11... | collective-permute-start | bytes 6291464 | tf_op jit(solution)/shard_map/ppermute | solution.py:356
  302.6 35.2 %collective-permute-start.74 = (bf16[768,512]{1,0:T(8,128)(2,1)S(1)}, bf16[768,512]{1,0:T(8,128)(2,1)S(1)}, u32[]{:S(2)}, u32[]{:S(2)}) collective-permute-start(bf16[768,512]{1,0:T(8,128)(2,1)S(1)} %get-tuple-element.90), channel_id=1, source_target_pairs={{0,4},{4,0},{8,12},{12,8},{16,20},{20,16},{24,28},{28,24},{1,5},{5... | collective-permute-start | bytes 2359304 | tf_op jit(solution)/shard_map/ppermute | solution.py:364
  305.5 34.4 %collective-permute-start.52 = (bf16[512,1024]{1,0:T(8,128)(2,1)S(1)}, bf16[512,1024]{1,0:T(8,128)(2,1)S(1)}, u32[]{:S(2)}, u32[]{:S(2)}) collective-permute-start(bf16[512,1024]{1,0:T(8,128)(2,1)S(1)} %slice.144), channel_id=1, source_target_pairs={{0,1},{1,0},{2,3},{3,2},{4,5},{5,4},{6,7},{7,6},{8,9},{9,8},{10,11... | collective-permute-start | bytes 3145736 | tf_op jit(solution)/shard_map/ppermute | solution.py:356
  308.5 35.3 %collective-permute-start.58 = (bf16[512,1024]{1,0:T(8,128)(2,1)S(1)}, bf16[512,1024]{1,0:T(8,128)(2,1)S(1)}, u32[]{:S(2)}, u32[]{:S(2)}) collective-permute-start(bf16[512,1024]{1,0:T(8,128)(2,1)S(1)} %add_convert_fusion.3), channel_id=1, source_target_pairs={{0,2},{1,3},{2,0},{3,1},{4,6},{5,7},{6,4},{7,5},{8,10},{9,11},{10,... | collective-permute-start | bytes 3145736 | tf_op jit(solution)/shard_map/ppermute | solution.py:353
  343.6 44.0 %collective-permute-start.53 = (bf16[512,1024]{1,0:T(8,128)(2,1)S(1)}, bf16[512,1024]{1,0:T(8,128)(2,1)}, u32[]{:S(2)}, u32[]{:S(2)}) collective-permute-start(bf16[512,1024]{1,0:T(8,128)(2,1)S(1)} %add_convert_fusion.4), channel_id=1, source_target_pairs={{0,2},{1,3},{2,0},{3,1},{4,6},{5,7},{6,4},{7,5},{8,10},{9,11},{10,... | collective-permute-start | bytes 3145736 | tf_op jit(solution)/shard_map/ppermute | solution.py:353
  343.7 43.9 %collective-permute-start.59 = (bf16[512,1024]{1,0:T(8,128)(2,1)S(1)}, bf16[512,1024]{1,0:T(8,128)(2,1)S(1)}, u32[]{:S(2)}, u32[]{:S(2)}) collective-permute-start(bf16[512,1024]{1,0:T(8,128)(2,1)S(1)} %collective-permute-done.58.refs_2_), channel_id=1, source_target_pairs={{0,1},{1,0},{2,3},{3,2},{4,5},{5,4},{6,7},{7,6},{8,9},{9,8},{10,11... | collective-permute-start | bytes 3145736 | tf_op jit(solution)/shard_map/ppermute | solution.py:356
  385.1 59.7 %collective-permute-start.49 = (bf16[1024,1024]{1,0:T(8,128)(2,1)S(1)}, bf16[1024,1024]{1,0:T(8,128)(2,1)}, u32[]{:S(2)}, u32[]{:S(2)}) collective-permute-start(bf16[1024,1024]{1,0:T(8,128)(2,1)S(1)} %copy-done.6), channel_id=1, source_target_pairs={{0,1},{1,0},{2,3},{3,2},{4,5},{5,4},{6,7},{7,6},{8,9},{9,8},{10,11... | collective-permute-start | bytes 6291464 | tf_op jit(solution)/shard_map/ppermute | solution.py:356
  387.6 57.6 %collective-permute-start.54 = (bf16[512,1024]{1,0:T(8,128)(2,1)}, bf16[512,1024]{1,0:T(8,128)(2,1)}, u32[]{:S(2)}, u32[]{:S(2)}) collective-permute-start(bf16[512,1024]{1,0:T(8,128)(2,1)} %collective-permute-done.53.refs_2_), channel_id=1, source_target_pairs={{0,1},{1,0},{2,3},{3,2},{4,5},{5,4},{6,7},{7,6},{8,9},{9,8},{10,11... | collective-permute-start | bytes 3145736 | tf_op jit(solution)/shard_map/ppermute | solution.py:356
  398.6 53.6 %collective-permute-start.69 = (bf16[512,512]{1,0:T(8,128)(2,1)}, bf16[512,512]{1,0:T(8,128)(2,1)}, u32[]{:S(2)}, u32[]{:S(2)}) collective-permute-start(bf16[512,512]{1,0:T(8,128)(2,1)} %get-tuple-element.86), channel_id=1, source_target_pairs={{0,2},{1,3},{2,0},{3,1},{4,6},{5,7},{6,4},{7,5},{8,10},{9,11},{10,... | collective-permute-start | bytes 1572872 | tf_op jit(solution)/shard_map/ppermute | solution.py:353
  398.7 58.3 %collective-permute-start.68 = (bf16[512,512]{1,0:T(8,128)(2,1)}, bf16[512,512]{1,0:T(8,128)(2,1)}, u32[]{:S(2)}, u32[]{:S(2)}) collective-permute-start(bf16[512,512]{1,0:T(8,128)(2,1)} %get-tuple-element.84), channel_id=1, source_target_pairs={{0,2},{1,3},{2,0},{3,1},{4,6},{5,7},{6,4},{7,5},{8,10},{9,11},{10,... | collective-permute-start | bytes 1572872 | tf_op jit(solution)/shard_map/ppermute | solution.py:353
  444.8 58.9 %collective-permute-start.62 = (bf16[1024,512]{1,0:T(8,128)(2,1)}, bf16[1024,512]{1,0:T(8,128)(2,1)}, u32[]{:S(2)}, u32[]{:S(2)}) collective-permute-start(bf16[1024,512]{1,0:T(8,128)(2,1)} %get-tuple-element.80), channel_id=1, source_target_pairs={{0,4},{4,0},{8,12},{12,8},{16,20},{20,16},{24,28},{28,24},{1,5},{5... | collective-permute-start | bytes 3145736 | tf_op jit(solution)/shard_map/ppermute | solution.py:364
  445.2 68.8 %collective-permute-start.60 = (bf16[1024,1024]{1,0:T(8,128)(2,1)}, bf16[1024,1024]{1,0:T(8,128)(2,1)}, u32[]{:S(2)}, u32[]{:S(2)}) collective-permute-start(bf16[1024,1024]{1,0:T(8,128)(2,1)} %convolution_convert_fusion.refs_0_), channel_id=1, source_target_pairs={{0,1},{1,0},{2,3},{3,2},{4,5},{5,4},{6,7},{7,6},{8,9},{9,8},{10,11... | collective-permute-start | bytes 6291464 | tf_op jit(solution)/shard_map/ppermute | solution.py:356
  453.4 34.7 %collective-permute-start.70 = (bf16[512,512]{1,0:T(8,128)(2,1)S(1)}, bf16[512,512]{1,0:T(8,128)(2,1)S(1)}, u32[]{:S(2)}, u32[]{:S(2)}) collective-permute-start(bf16[512,512]{1,0:T(8,128)(2,1)S(1)} %add_convert_fusion.9), channel_id=1, source_target_pairs={{0,4},{4,0},{8,12},{12,8},{16,20},{20,16},{24,28},{28,24},{1,5},{5... | collective-permute-start | bytes 1572872 | tf_op jit(solution)/shard_map/ppermute | solution.py:364
  455.4 37.0 %collective-permute-start.55 = (bf16[1024,256]{1,0:T(8,128)(2,1)S(1)}, bf16[1024,256]{1,0:T(8,128)(2,1)S(1)}, u32[]{:S(2)}, u32[]{:S(2)}) collective-permute-start(bf16[1024,256]{1,0:T(8,128)(2,1)S(1)} %get-tuple-element.65), channel_id=1, source_target_pairs={{0,2},{1,3},{2,0},{3,1},{4,6},{5,7},{6,4},{7,5},{8,10},{9,11},{10,... | collective-permute-start | bytes 1572872 | tf_op jit(solution)/shard_map/ppermute | solution.py:353
  457.0 46.7 %collective-permute-start.64 = (bf16[1024,512]{1,0:T(8,128)(2,1)S(1)}, bf16[1024,512]{1,0:T(8,128)(2,1)S(1)}, u32[]{:S(2)}, u32[]{:S(2)}) collective-permute-start(bf16[1024,512]{1,0:T(8,128)(2,1)S(1)} %add_convert_fusion.1), channel_id=1, source_target_pairs={{0,2},{1,3},{2,0},{3,1},{4,6},{5,7},{6,4},{7,5},{8,10},{9,11},{10,... | collective-permute-start | bytes 3145736 | tf_op jit(solution)/shard_map/ppermute | solution.py:353
  506.5 55.7 %collective-permute-start.65 = (bf16[1024,128]{1,0:T(8,128)(2,1)}, bf16[1024,128]{1,0:T(8,128)(2,1)S(1)}, u32[]{:S(2)}, u32[]{:S(2)}) collective-permute-start(bf16[1024,128]{1,0:T(8,128)(2,1)} %get-tuple-element.107), channel_id=1, source_target_pairs={{0,8},{4,12},{8,16},{12,20},{16,24},{20,28},{24,0},{28,4},{1,9},{5... | collective-permute-start | bytes 786440 | tf_op jit(solution)/shard_map/ppermute | solution.py:370
  509.6 52.6 %collective-permute-start.66 = (bf16[1024,128]{1,0:T(8,128)(2,1)}, bf16[1024,128]{1,0:T(8,128)(2,1)}, u32[]{:S(2)}, u32[]{:S(2)}) collective-permute-start(bf16[1024,128]{1,0:T(8,128)(2,1)} %get-tuple-element.109), channel_id=1, source_target_pairs={{0,16},{4,20},{8,24},{12,28},{16,0},{20,4},{24,8},{28,12},{1,17},{... | collective-permute-start | bytes 786440 | tf_op jit(solution)/shard_map/ppermute | solution.py:370
  511.1 51.2 %collective-permute-start.67 = (bf16[1024,128]{1,0:T(8,128)(2,1)}, bf16[1024,128]{1,0:T(8,128)(2,1)}, u32[]{:S(2)}, u32[]{:S(2)}) collective-permute-start(bf16[1024,128]{1,0:T(8,128)(2,1)} %get-tuple-element.108), channel_id=1, source_target_pairs={{0,24},{4,28},{8,0},{12,4},{16,8},{20,12},{24,16},{28,20},{1,25},{... | collective-permute-start | bytes 786440 | tf_op jit(solution)/shard_map/ppermute | solution.py:370
  (110 other events, 1451.7 us)
